TPU v7x, 256 devices: a whole 4x4x8 slice. The times are simulated.
256 devices in a mesh: section: 8 (over x, y_hi), fsdp: 32 (over y_lo, z, core).
Axes of the slice: x: 4, y: 4 (y_hi: 2, y_lo: 2; y = y_hi * 2 + y_lo), z: 8, core: 2. Of those that a mesh axis runs over, the one named last changes fastest.
Arguments:
- fwd_first: bfloat16 [8, 3584, 3072], P('section', 'fsdp'), may hold values from -6 to 6
- fwd_second: bfloat16 [8, 3584, 3072], P('section', 'fsdp'), may hold values from -6 to 6
- bwd_first: bfloat16 [8, 3584, 3072], P('section', 'fsdp'), may hold values from -6 to 6
- bwd_second: bfloat16 [8, 3584, 3072], P('section', 'fsdp'), may hold values from -6 to 6
- grad_first: bfloat16 [8, 3584, 3072], P('section', 'fsdp'), may hold values from -6 to 6
- grad_second: bfloat16 [8, 3584, 3072], P('section', 'fsdp'), may hold values from -6 to 6
- w_query: bfloat16 [8, 3072, 256], P('section', 'fsdp'), may hold values from -0.109375 to 0.109375
- w_key: bfloat16 [8, 3072, 256], P('section', 'fsdp'), may hold values from -0.109375 to 0.109375
- w_value: bfloat16 [8, 3072, 256], P('section', 'fsdp'), may hold values from -0.109375 to 0.109375
- w_out: bfloat16 [8, 256, 3072], P('section', None, 'fsdp'), may hold values from -0.375 to 0.375
Outputs:
- next_first: bfloat16 [8, 3584, 3072], P('section', 'fsdp')
- next_second: bfloat16 [8, 3584, 3072], P('section', 'fsdp')
- back_first: bfloat16 [8, 3584, 3072], P('section', 'fsdp')
- back_second: bfloat16 [8, 3584, 3072], P('section', 'fsdp')
- back_grad_first: bfloat16 [8, 3584, 3072], P('section', 'fsdp')
- back_grad_second: bfloat16 [8, 3584, 3072], P('section', 'fsdp')
- query_weight_grad: float32 [8, 3072, 256], P('section', 'fsdp')
- key_weight_grad: float32 [8, 3072, 256], P('section', 'fsdp')
- value_weight_grad: float32 [8, 3072, 256], P('section', 'fsdp')
- out_weight_grad: float32 [8, 256, 3072], P('section', None, 'fsdp')
All inputs are finite; a program needn't handle non-finite values.
Results may differ from a plain program's by a relative error of at most 0.035.
Values may be sent and summed in bfloat16 or wider, within the bound.
No kernel may reach another device: no remote copies, remote signals or barrier semaphores. Data moves between devices by JAX's collectives and lax.ppermute only.
A program may use at most 128 MiB of HBM per device.

v0:
```python
import functools
import math

import jax
import jax.numpy as jnp
import numpy as np
from jax import lax
from jax.experimental import pallas as pl
from jax.experimental.pallas import tpu as pltpu
from jax.sharding import Mesh
from jax.sharding import PartitionSpec as P

HEADS = 2
HEAD_DIM = 128
Y, Z, C = 2, 8, 2
NEG = -1e30
SCALE = 1.0 / math.sqrt(HEAD_DIM)
F32 = jnp.float32
BF16 = jnp.bfloat16

epsilon = 1e-05


def passed_along(value, steps):
    count = lax.axis_size("section")
    first, last = (max(0, -steps), min(count, count - steps))
    return lax.ppermute(
        value, "section", [(source, source + steps) for source in range(first, last)]
    )


def swap(value, axis):
    return lax.ppermute(value, axis, [(0, 1), (1, 0)])


def ring(value, step):
    return lax.ppermute(value, "z", [(i, (i + step) % Z) for i in range(Z)])


def ring_gather(block, beside):
    beside = dict(beside)
    half = block.shape[0] // 2
    blocks = {0: block}
    ahead = behind = block
    for distance in range(1, Z // 2 + 1):
        if distance in beside:
            ahead, behind, beside[distance] = lax.optimization_barrier(
                (ahead, behind, beside[distance])
            )
        if distance == Z // 2:
            break
        ahead, behind = ring(ahead, -1), ring(behind, 1)
        blocks[distance], blocks[-distance] = ahead, behind
    blocks[Z // 2] = jnp.concatenate([ring(ahead[:half], -1), ring(behind[half:], 1)], axis=0)
    return blocks, beside


def ring_reduce(parts, beside):
    beside = dict(beside)
    half = parts[0].shape[0] // 2
    far = parts[Z // 2].astype(BF16)
    ahead = ring(far[:half], 1).astype(F32)
    behind = ring(far[half:], -1).astype(F32)
    last = Z // 2 - 1
    ahead = jnp.concatenate([parts[last][:half] + ahead, parts[last][half:]], axis=0)
    behind = jnp.concatenate([parts[-last][:half], parts[-last][half:] + behind], axis=0)
    for distance in range(last, 0, -1):
        if distance in beside:
            ahead, behind, beside[distance] = lax.optimization_barrier(
                (ahead, behind, beside[distance])
            )
        ahead = ring(ahead.astype(BF16), 1).astype(F32)
        behind = ring(behind.astype(BF16), -1).astype(F32)
        if distance > 1:
            ahead = ahead + parts[distance - 1]
            behind = behind + parts[1 - distance]
    return parts[0].astype(F32) + ahead + behind, beside


def inverse_rms(inputs):
    widened = inputs.astype(F32)
    return lax.rsqrt(jnp.mean(widened * widened, axis=-1, keepdims=True) + epsilon)


def dot(left, right, left_dim=1, right_dim=0):
    return lax.dot_general(
        left, right, (((left_dim,), (right_dim,)), ((), ())), preferred_element_type=F32
    )


def softmax_parts(scores, mask):
    scores = jnp.where(mask, scores, NEG)
    highest = jnp.max(scores, axis=-1, keepdims=True)
    weights = jnp.where(mask, jnp.exp(scores - highest), 0.0)
    return weights, highest, jnp.sum(weights, axis=-1, keepdims=True)


def statistics_kernel(chunk, q_b, g_b, q_f, kv, query_at, key_at, stats, out_f):
    def step(index, carry):
        rows = pl.ds(pl.multiple_of(index * chunk, chunk), chunk)
        mask = key_at[...] <= query_at[rows, :]
        weights, highest, total = softmax_parts(
            dot(q_b[rows, :], kv[:, :HEAD_DIM], 1, 1) * SCALE, mask
        )
        prob_grad = dot(g_b[rows, :], kv[:, HEAD_DIM : 2 * HEAD_DIM], 1, 1)
        stats[rows, 0:1] = highest
        stats[rows, 1:2] = total
        stats[rows, 2:3] = jnp.sum(weights * prob_grad, axis=-1, keepdims=True)
        weights, highest, total = softmax_parts(
            dot(q_f[rows, :], kv[:, 2 * HEAD_DIM : 3 * HEAD_DIM], 1, 1) * SCALE, mask
        )
        stats[rows, 3:4] = highest
        stats[rows, 4:5] = total
        out_f[rows, :] = dot(weights.astype(BF16), kv[:, 3 * HEAD_DIM :])
        return carry

    lax.fori_loop(0, q_b.shape[0] // chunk, step, 0)


def gradients_kernel(chunk, q_b, g_b, kv, query_at, key_at, scales, out_rows, out_kv):
    out_kv[...] = jnp.zeros_like(out_kv)

    def step(index, carry):
        rows = pl.ds(pl.multiple_of(index * chunk, chunk), chunk)
        mask = key_at[...] <= query_at[rows, :]
        queries, grads = q_b[rows, :], g_b[rows, :]
        keys, values = kv[:, :HEAD_DIM], kv[:, HEAD_DIM : 2 * HEAD_DIM]
        scores = jnp.where(mask, dot(queries, keys, 1, 1) * SCALE, NEG)
        probs = jnp.where(mask, jnp.exp(scores - scales[rows, 0:1]), 0.0) * scales[rows, 1:2]
        prob_grad = dot(grads, values, 1, 1)
        score_grad = (probs * (prob_grad - scales[rows, 2:3]) * SCALE).astype(BF16)
        probs_half = probs.astype(BF16)
        out_rows[rows, :HEAD_DIM] = dot(score_grad, keys)
        out_rows[rows, HEAD_DIM:] = dot(probs_half, values)
        out_kv[:, :HEAD_DIM] += dot(score_grad, queries, 0, 0)
        out_kv[:, HEAD_DIM:] += dot(probs_half, grads, 0, 0)
        return carry

    lax.fori_loop(0, q_b.shape[0] // chunk, step, 0)


def kernel_call(kernel, chunk, outs, products, exps, operands):
    rows, keys = operands[0].shape[0], Z * operands[0].shape[0] // 2
    return pl.pallas_call(
        functools.partial(kernel, chunk),
        out_shape=[jax.ShapeDtypeStruct(shape, F32) for shape in outs],
        compiler_params=pltpu.CompilerParams(vmem_limit_bytes=32 * 1024 * 1024),
        cost_estimate=pl.CostEstimate(
            flops=2 * products * rows * keys * HEAD_DIM,
            bytes_accessed=sum(operand.size * operand.dtype.itemsize for operand in operands),
            transcendentals=exps * rows * keys,
        ),
    )(*operands)


def merged(highest, total, other_highest, other_total):
    top = jnp.maximum(highest, other_highest)
    own = jnp.exp(highest - top)
    other = jnp.exp(other_highest - top)
    whole = total * own + other_total * other
    inverse = 1.0 / jnp.where(whole > 0.0, whole, 1.0)
    return top, inverse, own * inverse, other * inverse


def per_device(
    fwd_first,
    fwd_second,
    bwd_first,
    bwd_second,
    grad_first,
    grad_second,
    w_query,
    w_key,
    w_value,
    w_out,
):
    c, y, z = lax.axis_index("c"), lax.axis_index("yl"), lax.axis_index("z")
    tokens = fwd_first.shape[1]
    chip = C * tokens
    stream_f, stream_b, cot_out = fwd_second[0], bwd_first[0], grad_second[0]

    wide = 2 * HEAD_DIM
    out_rows = w_out[0].T

    def by_core(own, other):
        return jnp.where(
            c == 0,
            jnp.concatenate([own, other], axis=0),
            jnp.concatenate([other, own], axis=0),
        )

    by_head = [
        jnp.concatenate(
            [
                part[:, head * HEAD_DIM : (head + 1) * HEAD_DIM]
                for part in (w_key[0], w_value[0], w_query[0], out_rows)
            ],
            axis=1,
        )
        for head in range(HEADS)
    ]
    mine = jnp.where(c == 0, by_head[0], by_head[1])
    given_away = jnp.where(c == 0, by_head[1], by_head[0])
    mine, given_away, stream_f, stream_b, cot_out = lax.optimization_barrier(
        (mine, given_away, stream_f, stream_b, cot_out)
    )
    block = by_core(mine, swap(given_away, "c"))
    other_block = by_core(
        swap(mine, "yl"),
        lax.ppermute(given_away, ("yl", "c"), [(i, Y * C - 1 - i) for i in range(Y * C)]),
    )
    pair = jnp.where(y == 0, jnp.stack([block, other_block]), jnp.stack([other_block, block]))

    stream_bg = jnp.concatenate([stream_b, cot_out], axis=0)
    other_f, other_bg = swap(stream_f, "c"), swap(stream_bg, "c")
    pair, early_f, early_bg = lax.optimization_barrier((pair, stream_f, stream_bg))
    next_first = passed_along(early_f, 1)
    back_both = passed_along(early_bg, -1)

    both_f = jnp.concatenate([stream_f, other_f], axis=0)
    both_b = jnp.concatenate([stream_b, other_bg[:tokens]], axis=0)
    both_g = jnp.concatenate([cot_out, other_bg[tokens:]], axis=0)
    inverse_b, inverse_f = inverse_rms(both_b), inverse_rms(both_f)
    half_b = (both_b.astype(F32) * inverse_b).astype(BF16)
    half_f = (both_f.astype(F32) * inverse_f).astype(BF16)

    w_kvqo = lax.all_gather(pair, "z", axis=1).reshape(-1, 2 * wide)
    w_kvq, w_o = w_kvqo[:, : 3 * HEAD_DIM], w_kvqo[:, 3 * HEAD_DIM :]

    half = jnp.concatenate([half_b, half_f], axis=0)
    kv_all = dot(half, w_kvqo[:, :wide]).astype(BF16)
    kv_own = jnp.concatenate([kv_all[:chip], kv_all[chip:]], axis=1)

    def heads_together(own, other):
        return jnp.where(
            c == 0,
            jnp.concatenate([own, other], axis=1),
            jnp.concatenate([other, own], axis=1),
        )

    section = lax.axis_index("section")

    def after_first(value):
        return jnp.where(section > 0, value, jnp.zeros_like(value))[None]

    def before_last(value):
        return jnp.where(
            section < lax.axis_size("section") - 1, value, jnp.zeros_like(value)
        )[None]

    def lend(value):
        return lax.ppermute(value, "yl", [(1, 0)])

    def give_back(value):
        return lax.ppermute(value, "yl", [(0, 1)])

    order = [0] + [d for k in range(1, Z // 2) for d in (k, -k)] + [Z // 2]
    spot = jnp.arange(Z * chip, dtype=jnp.int32)
    inside = spot % chip
    inside = jnp.where(
        inside < tokens, inside + c * tokens, inside + (1 - c) * tokens - tokens
    )
    distances = jnp.asarray(np.repeat(np.array(order, np.int32), chip))
    key_index = ((y * Z + (z + distances) % Z) * chip + inside).astype(jnp.int32)
    spot = jnp.arange(2 * chip, dtype=jnp.int32)
    inside = spot % chip
    inside = jnp.where(
        inside < tokens, inside + c * tokens, inside + (1 - c) * tokens - tokens
    )
    query_index = (jnp.where(spot < chip, y, 1 - y) * Z + z) * chip + inside
    key_at, query_at = key_index[None, :], query_index[:, None]

    blocks, beside = ring_gather(
        kv_own, {2: (half, both_g), 4: (next_first, back_both)}
    )
    half_late, both_g_late = beside[2]
    next_first, back_both = beside[4]
    q_all = dot(half_late, w_kvqo[:, wide : 3 * HEAD_DIM]).astype(BF16)
    q_b, q_f = q_all[:chip], q_all[chip:]
    da_b = dot(both_g_late, w_o).astype(BF16)
    lent = lend(jnp.concatenate([q_b, da_b, q_f], axis=1))
    blocks[Z // 2], lent = lax.optimization_barrier((blocks[Z // 2], lent))
    queries_b, grads_b, queries_f = (
        jnp.concatenate([own, lent[:, k * HEAD_DIM : (k + 1) * HEAD_DIM]], axis=0)
        for k, own in enumerate((q_b, da_b, q_f))
    )
    kv = jnp.concatenate([blocks[d] for d in order], axis=0)
    def exchanged(columns):
        stats = jnp.concatenate(columns, axis=1)
        sent = jnp.where(y == 0, stats[chip:], stats[:chip])
        received = swap(sent, "yl")
        none = jnp.concatenate(
            [jnp.full((chip, 1), NEG, F32), jnp.zeros((chip, len(columns) - 1), F32)], axis=1
        )
        full = jnp.where(
            y == 0,
            jnp.concatenate([none, received], axis=0),
            jnp.concatenate([received, none], axis=0),
        )
        return [full[:, k : k + 1] for k in range(len(columns))]

    stats, out_f = kernel_call(
        statistics_kernel,
        tokens,
        [(2 * chip, 8), (2 * chip, HEAD_DIM)],
        4,
        2,
        (queries_b, grads_b, queries_f, kv, query_at, key_at),
    )
    highest, total, row_part, highest_f, total_f = (stats[:, k : k + 1] for k in range(5))
    other_highest, other_total, other_row, other_highest_f, other_total_f = exchanged(
        [highest, total, row_part, highest_f, total_f]
    )
    top, inverse, own_scale, other_scale = merged(highest, total, other_highest, other_total)
    own_scale_f = merged(highest_f, total_f, other_highest_f, other_total_f)[2]
    row_dot = row_part * own_scale + other_row * other_scale
    rows_b, kv_part = kernel_call(
        gradients_kernel,
        tokens,
        [(2 * chip, wide), (Z * chip, wide)],
        6,
        1,
        (
            queries_b,
            grads_b,
            kv,
            query_at,
            key_at,
            jnp.concatenate([top, inverse, row_dot], axis=1),
        ),
    )
    def given(rows):
        return rows[:chip] + give_back(rows[chip:].astype(BF16)).astype(F32)

    def projected(attended, received):
        return dot(attended[:tokens], w_o, 1, 1) + received.astype(F32)

    def for_other_core(attended):
        return swap(dot(attended[tokens:], w_o, 1, 1).astype(BF16), "c")

    attended_f = given(out_f * own_scale_f).astype(BF16)
    received_f = for_other_core(attended_f)
    updated = (fwd_first[0].astype(F32) + projected(attended_f, received_f)).astype(BF16)

    next_second = passed_along(updated, 1)

    own_rows = given(rows_b)
    q_grad, attended_b = own_rows[:, :HEAD_DIM].astype(BF16), own_rows[:, HEAD_DIM:].astype(BF16)
    received_b = for_other_core(attended_b)
    rec_first = (bwd_second[0].astype(F32) - projected(attended_b, received_b)).astype(BF16)

    kv_grad, beside = ring_reduce(
        {d: kv_part[i * chip : (i + 1) * chip] for i, d in enumerate(order)},
        {1: (rec_first,)},
    )
    (rec_first,) = beside[1]
    kv_grad = kv_grad.astype(BF16)
    back_first = passed_along(rec_first, -1)

    grads = jnp.concatenate([kv_grad, q_grad], axis=1)
    grads_late, next_second = lax.optimization_barrier((grads, next_second))
    received = swap(dot(grads_late[tokens:], w_kvq, 1, 1).astype(BF16), "c")
    normed_grad = dot(grads_late[:tokens], w_kvq, 1, 1) + received.astype(F32)
    normed_own, inverse_own = stream_b.astype(F32) * inverse_b[:tokens], inverse_b[:tokens]
    input_grad = inverse_own * (
        normed_grad - normed_own * jnp.mean(normed_grad * normed_own, axis=-1, keepdims=True)
    )
    cot_second = (grad_first[0].astype(F32) + input_grad).astype(BF16)

    zeros = jnp.zeros_like(q_grad)
    wpart = dot(
        jnp.concatenate([half_b, both_g], axis=0),
        jnp.concatenate(
            [
                jnp.concatenate([grads, zeros], axis=1),
                jnp.concatenate([zeros, zeros, zeros, attended_b], axis=1),
            ],
            axis=0,
        ),
        0,
        0,
    ).astype(BF16)
    by_chip = wpart.reshape(Y, Z, -1, 2 * wide).transpose(1, 0, 2, 3)
    over_z = lax.psum_scatter(
        by_chip.reshape(-1, 2 * wide), "z", scatter_dimension=0, tiled=True
    )
    cot_second, next_first, back_both = lax.optimization_barrier(
        (cot_second, next_first, back_both)
    )
    back_grad_second = passed_along(cot_second, -1)
    next_first = after_first(next_first)
    back_second, back_grad_first = before_last(back_both[:tokens]), before_last(back_both[tokens:])
    over_z, next_first, back_second, back_grad_first, next_second, back_first, back_grad_second = (
        lax.optimization_barrier(
            (
                over_z,
                next_first,
                back_second,
                back_grad_first,
                next_second,
                back_first,
                back_grad_second,
            )
        )
    )
    rows = over_z.shape[0] // (Y * C)
    corner = over_z.astype(F32).reshape(Y, C, rows, 2 * wide)

    def of(y_, c_):
        return lax.dynamic_slice(corner, (y_, c_, 0, 0), (1, 1, rows, 2 * wide))[0, 0]

    def of_other(c_):
        return of(1 - y, c_).astype(BF16)

    across = lax.ppermute(
        of_other(1 - c), ("yl", "c"), [(i, Y * C - 1 - i) for i in range(Y * C)]
    ).astype(F32)
    own = of(y, c) + swap(of_other(c), "yl").astype(F32)
    other = swap(of(y, 1 - c).astype(BF16), "c").astype(F32) + across

    def heads_of(index):
        span = slice(index * HEAD_DIM, (index + 1) * HEAD_DIM)
        return heads_together(own[:, span], other[:, span])

    return (
        next_first,
        after_first(next_second),
        before_last(back_first),
        back_second,
        back_grad_first,
        before_last(back_grad_second),
        heads_of(2)[None],
        heads_of(0)[None],
        heads_of(1)[None],
        heads_of(3).T[None],
    )


def solution(mesh):
    sections = mesh.devices.shape[0]
    split = Mesh(mesh.devices.reshape(sections, Y, Z, C), ("section", "yl", "z", "c"))
    fsdp = ("yl", "z", "c")
    rows = P("section", fsdp, None)
    columns = P("section", None, fsdp)
    return jax.shard_map(
        per_device,
        mesh=split,
        in_specs=(rows,) * 9 + (columns,),
        out_specs=(rows,) * 9 + (columns,),
        check_vma=False,
    )
```

profile of v0, /device:TPU:19, one launch (start us, length us, event | category | flops | bytes accessed | tf_op | source)
XLA Modules:
  0.0 242.0 jit_solution(11631602607958769834)
XLA Ops:
  7.2 0.8 fusion.82
  8.1 0.8 fusion.83
  8.8 0.8 fusion.84
  10.4 1.6 collective-permute-start.4
  12.5 2.0 constant_dynamic-update-slice_fusion.1
  14.5 0.9 constant_dynamic-update-slice_fusion
  15.4 2.5 %collective-permute-done.3 = bf16[96,512]{1,0:T(8,128)(2,1)S(1)} collective-permute-done((bf16[96,512]{1,0:T(8,128)(2,1)S(1)}, bf16[96,512]{1,0:T(8,128)(2,1)S(1)}, u32[]{:S(2)}, u32[]{:S(2)}) %collective-permute-start.3) | collective-permute-done | bytes 98336 | tf_op jit(solution)/shard_map/ppermute | solution.py:33
  18.0 0.8 maximum_select_fusion
  19.7 2.0 collective-permute-start.12
  21.7 5.7 %collective-permute-start.11 = (bf16[112,3072]{1,0:T(8,128)(2,1)S(1)}, bf16[112,3072]{1,0:T(8,128)(2,1)}, u32[]{:S(2)}, u32[]{:S(2)}) collective-permute-start(bf16[112,3072]{1,0:T(8,128)(2,1)S(1)} %bitcast.84), channel_id=1, source_target_pairs={{0,32},{32,64},{64,96},{96,128},{128,160},{160,192},{192,224},{1,3... | collective-permute-start | bytes 2064392 | tf_op jit(solution)/shard_map/ppermute | solution.py:27
  28.2 0.9 fusion.74
  30.6 1.8 pad_maximum_fusion
  32.4 33.9 %all-gather.3.cloned.1.call-done = bf16[2,1536,512]{2,1,0:T(8,128)(2,1)} async-done(((bf16[2,192,512]{2,1,0:T(8,128)(2,1)}), bf16[2,1536,512]{2,1,0:T(8,128)(2,1)}) %all-gather.3.cloned.1.call-update) | async-done | bytes 3145744 | tf_op jit(solution)/shard_map/all_gather | solution.py:227
  66.3 2.8 %fusion.17 = bf16[448,256]{1,0:T(8,128)(2,1)S(1)} fusion(bf16[3072,512]{1,0:T(8,128)(2,1)} %bitcast.73, bf16[224,3072]{1,0:T(8,128)(2,1)S(1)} %fusion.7, bf16[224,3072]{1,0:T(8,128)(2,1)} %copy-done.3), kind=kOutput, calls=%fused_computation.35 | convolution fusion | flops 710262784 | bytes 4554752 | tf_op jit(solution)/shard_map/dot_general | solution.py:86
  69.2 1.2 collective-permute-start.5
  70.9 4.6 %collective-permute-done.5 = bf16[224,512]{1,0:T(8,128)(2,1)S(1)} collective-permute-done((bf16[224,512]{1,0:T(8,128)(2,1)S(1)}, bf16[224,512]{1,0:T(8,128)(2,1)S(1)}, u32[]{:S(2)}, u32[]{:S(2)}) %collective-permute-start.5) | collective-permute-done | bytes 229408 | tf_op jit(solution)/shard_map/ppermute | solution.py:37
  75.5 1.6 collective-permute-done.6
  77.7 0.9 convolution_convert_fusion.4
  78.6 1.3 collective-permute-start.15
  80.0 2.7 %collective-permute-start.7 = (bf16[224,512]{1,0:T(8,128)(2,1)S(1)}, bf16[224,512]{1,0:T(8,128)(2,1)S(1)}, u32[]{:S(2)}, u32[]{:S(2)}) collective-permute-start(bf16[224,512]{1,0:T(8,128)(2,1)S(1)} %collective-permute-done.5), channel_id=1, source_target_pairs={{0,14},{2,0},{4,2},{6,4},{8,6},{10,8},{12,10},{14,12},{1,15},{3,1}... | collective-permute-start | bytes 688136 | tf_op jit(solution)/shard_map/ppermute | solution.py:37
  82.7 3.4 %collective-permute-done.9 = bf16[224,512]{1,0:T(8,128)(2,1)S(1)} collective-permute-done((bf16[224,512]{1,0:T(8,128)(2,1)S(1)}, bf16[224,512]{1,0:T(8,128)(2,1)S(1)}, u32[]{:S(2)}, u32[]{:S(2)}) %collective-permute-start.9) | collective-permute-done | bytes 229408 | tf_op jit(solution)/shard_map/ppermute | solution.py:37
  86.1 2.7 %collective-permute-start.8 = (bf16[224,512]{1,0:T(8,128)(2,1)S(1)}, bf16[224,512]{1,0:T(8,128)(2,1)S(1)}, u32[]{:S(2)}, u32[]{:S(2)}) collective-permute-start(bf16[224,512]{1,0:T(8,128)(2,1)S(1)} %collective-permute-done.7), channel_id=1, source_target_pairs={{0,14},{2,0},{4,2},{6,4},{8,6},{10,8},{12,10},{14,12},{1,15},{3,1}... | collective-permute-start | bytes 688136 | tf_op jit(solution)/shard_map/ppermute | solution.py:37
  88.8 3.3 %collective-permute-done.10 = bf16[224,512]{1,0:T(8,128)(2,1)S(1)} collective-permute-done((bf16[224,512]{1,0:T(8,128)(2,1)S(1)}, bf16[224,512]{1,0:T(8,128)(2,1)S(1)}, u32[]{:S(2)}, u32[]{:S(2)}) %collective-permute-start.10) | collective-permute-done | bytes 229408 | tf_op jit(solution)/shard_map/ppermute | solution.py:37
  92.2 2.8 %collective-permute-start.13 = (bf16[112,512]{1,0:T(8,128)(2,1)S(1)}, bf16[112,512]{1,0:T(8,128)(2,1)S(1)}, u32[]{:S(2)}, u32[]{:S(2)}) collective-permute-start(bf16[112,512]{1,0:T(8,128)(2,1)S(1)} %slice.245), channel_id=1, source_target_pairs={{0,14},{2,0},{4,2},{6,4},{8,6},{10,8},{12,10},{14,12},{1,15},{3,1}... | collective-permute-start | bytes 344072 | tf_op jit(solution)/shard_map/ppermute | solution.py:37
  95.1 2.3 collective-permute-done.13
  97.4 2.5 %collective-permute-done.14 = bf16[112,512]{1,0:T(8,128)(2,1)S(1)} collective-permute-done((bf16[112,512]{1,0:T(8,128)(2,1)S(1)}, bf16[112,512]{1,0:T(8,128)(2,1)S(1)}, u32[]{:S(2)}, u32[]{:S(2)}) %collective-permute-start.14) | collective-permute-done | bytes 114720 | tf_op jit(solution)/shard_map/ppermute | solution.py:37
  100.0 5.2 %shard_map.186 = (f32[448,8]{1,0:T(8,128)S(1)}, f32[448,128]{1,0:T(8,128)S(1)}) custom-call(bf16[448,128]{1,0:T(8,128)(2,1)S(1)} %pad_maximum_fusion.10.q_b, bf16[448,128]{1,0:T(8,128)(2,1)S(1)} %pad_maximum_fusion.11.g_b, bf16[448,128]{1,0:T(8,128)(2,1)S(1)} %pad_maximum_fusion.12.q_f, bf16[1792,512]{1,0:T(8,128)(2,1)S(1)} %constant_dynamic-update-slice_fusion.2.kv, ...), custom_call_target="tpu_custom_call" | custom-call | flops 822083584 | bytes 2188032 | tf_op jit(solution)/shard_map/pallas_call | solution.py:144
  105.3 2.1 collective-permute-start.16
  107.4 2.2 collective-permute-done.16
  110.5 4.4 %shard_map.187 = (f32[448,256]{1,0:T(8,128)S(1)}, f32[1792,256]{1,0:T(8,128)S(1)}) custom-call(bf16[448,128]{1,0:T(8,128)(2,1)S(1)} %pad_maximum_fusion.10.q_b, bf16[448,128]{1,0:T(8,128)(2,1)S(1)} %pad_maximum_fusion.11.g_b, bf16[1792,512]{1,0:T(8,128)(2,1)S(1)} %constant_dynamic-update-slice_fusion.2.kv, s32[448,1]{1,0:T(8,128)S(1)} %select_add_fusion.query_at, ...), custom_call_target="tpu_custom_call" | custom-call | flops 1233125376 | bytes 2078720 | tf_op jit(solution)/shard_map/pallas_call | solution.py:144
  115.1 2.7 %collective-permute-start.20 = (bf16[112,256]{1,0:T(8,128)(2,1)S(1)}, bf16[112,256]{1,0:T(8,128)(2,1)S(1)}, u32[]{:S(2)}, u32[]{:S(2)}) collective-permute-start(bf16[112,256]{1,0:T(8,128)(2,1)S(1)} %get-tuple-element.98), channel_id=1, source_target_pairs={{0,14},{2,0},{4,2},{6,4},{8,6},{10,8},{12,10},{14,12},{1,15},{3,1}... | collective-permute-start | bytes 172040 | tf_op jit(solution)/shard_map/ppermute | solution.py:37
  117.8 3.4 %collective-permute-start.23 = (bf16[224,256]{1,0:T(8,128)(2,1)S(1)}, bf16[224,256]{1,0:T(8,128)(2,1)S(1)}, u32[]{:S(2)}, u32[]{:S(2)}) collective-permute-start(bf16[224,256]{1,0:T(8,128)(2,1)S(1)} %slice.432), channel_id=1, source_target_pairs={{0,16},{1,17},{2,18},{3,19},{4,20},{5,21},{6,22},{7,23},{8,24},{9,... | collective-permute-start | bytes 344072 | tf_op jit(solution)/shard_map/ppermute | solution.py:255
  121.4 2.7 %collective-permute-start.21 = (bf16[224,256]{1,0:T(8,128)(2,1)S(1)}, bf16[224,256]{1,0:T(8,128)(2,1)S(1)}, u32[]{:S(2)}, u32[]{:S(2)}) collective-permute-start(bf16[224,256]{1,0:T(8,128)(2,1)S(1)} %pad_maximum_fusion.14), channel_id=1, source_target_pairs={{0,14},{2,0},{4,2},{6,4},{8,6},{10,8},{12,10},{14,12},{1,15},{3,1}... | collective-permute-start | bytes 344072 | tf_op jit(solution)/shard_map/ppermute | solution.py:37
  124.5 10.4 %collective-permute-start.24 = (bf16[112,3072]{1,0:T(8,128)(2,1)S(1)}, bf16[112,3072]{1,0:T(8,128)(2,1)S(1)}, u32[]{:S(2)}, u32[]{:S(2)}) collective-permute-start(bf16[112,3072]{1,0:T(8,128)(2,1)S(1)} %convolution_convert_fusion.3), channel_id=1, source_target_pairs={{0,1},{1,0},{2,3},{3,2},{4,5},{5,4},{6,7},{7,6},{8,9},{9,8},{10,11... | collective-permute-start | bytes 2064392 | tf_op jit(solution)/shard_map/ppermute | solution.py:33
  135.0 2.7 %collective-permute-start.22 = (bf16[224,256]{1,0:T(8,128)(2,1)S(1)}, bf16[224,256]{1,0:T(8,128)(2,1)S(1)}, u32[]{:S(2)}, u32[]{:S(2)}) collective-permute-start(bf16[224,256]{1,0:T(8,128)(2,1)S(1)} %get-tuple-element.89), channel_id=1, source_target_pairs={{0,14},{2,0},{4,2},{6,4},{8,6},{10,8},{12,10},{14,12},{1,15},{3,1}... | collective-permute-start | bytes 344072 | tf_op jit(solution)/shard_map/ppermute | solution.py:37
  137.7 2.2 collective-permute-done.19
  140.7 2.7 %collective-permute-start.26 = (bf16[224,256]{1,0:T(8,128)(2,1)S(1)}, bf16[224,256]{1,0:T(8,128)(2,1)S(1)}, u32[]{:S(2)}, u32[]{:S(2)}) collective-permute-start(bf16[224,256]{1,0:T(8,128)(2,1)S(1)} %get-tuple-element.67), channel_id=1, source_target_pairs={{0,14},{2,0},{4,2},{6,4},{8,6},{10,8},{12,10},{14,12},{1,15},{3,1}... | collective-permute-start | bytes 344072 | tf_op jit(solution)/shard_map/ppermute | solution.py:37
  143.4 2.1 collective-permute-done.25
  145.6 1.9 convolution_convert_fusion
  147.4 1.9 copy.40
  149.5 3.0 %collective-permute-start.27 = (bf16[224,128]{1,0:T(8,128)(2,1)S(1)}, bf16[224,128]{1,0:T(8,128)(2,1)S(1)}, u32[]{:S(2)}, u32[]{:S(2)}) collective-permute-start(bf16[224,128]{1,0:T(8,128)(2,1)S(1)} %slice.433), channel_id=1, source_target_pairs={{0,16},{1,17},{2,18},{3,19},{4,20},{5,21},{6,22},{7,23},{8,24},{9,... | collective-permute-start | bytes 172040 | tf_op jit(solution)/shard_map/ppermute | solution.py:255
  152.6 1.2 collective-permute-done.27
  153.8 1.5 convolution_convert_fusion.2
  155.3 6.2 %collective-permute-start.28 = (bf16[112,3072]{1,0:T(8,128)(2,1)S(1)}, bf16[112,3072]{1,0:T(8,128)(2,1)S(1)}, u32[]{:S(2)}, u32[]{:S(2)}) collective-permute-start(bf16[112,3072]{1,0:T(8,128)(2,1)S(1)} %convolution_convert_fusion.2), channel_id=1, source_target_pairs={{0,1},{1,0},{2,3},{3,2},{4,5},{5,4},{6,7},{7,6},{8,9},{9,8},{10,11... | collective-permute-start | bytes 2064392 | tf_op jit(solution)/shard_map/ppermute | solution.py:33
  161.6 1.8 collective-permute-done.28
  163.4 1.5 fusion.3
  164.9 3.0 %collective-permute-start.29 = (bf16[112,3072]{1,0:T(8,128)(2,1)S(1)}, bf16[112,3072]{1,0:T(8,128)(2,1)S(1)}, u32[]{:S(2)}, u32[]{:S(2)}) collective-permute-start(bf16[112,3072]{1,0:T(8,128)(2,1)S(1)} %fusion.3), channel_id=1, source_target_pairs={{0,32},{32,64},{64,96},{96,128},{128,160},{160,192},{192,224},{1,3... | collective-permute-start | bytes 2064392 | tf_op jit(solution)/shard_map/ppermute | solution.py:27
  168.0 17.1 %collective-permute-done.29 = bf16[112,3072]{1,0:T(8,128)(2,1)S(1)} collective-permute-done((bf16[112,3072]{1,0:T(8,128)(2,1)S(1)}, bf16[112,3072]{1,0:T(8,128)(2,1)S(1)}, u32[]{:S(2)}, u32[]{:S(2)}) %collective-permute-start.29) | collective-permute-done | bytes 688160 | tf_op jit(solution)/shard_map/ppermute | solution.py:27
  185.0 1.7 convolution_convert_fusion.1
  186.8 1.1 collective-permute-start.30
  187.9 3.1 %collective-permute-start.31 = (bf16[112,3072]{1,0:T(8,128)(2,1)S(1)}, bf16[112,3072]{1,0:T(8,128)(2,1)S(1)}, u32[]{:S(2)}, u32[]{:S(2)}) collective-permute-start(bf16[112,3072]{1,0:T(8,128)(2,1)S(1)} %fusion.2), channel_id=1, source_target_pairs={{32,0},{64,32},{96,64},{128,96},{160,128},{192,160},{224,192},{33,... | collective-permute-start | bytes 2064392 | tf_op jit(solution)/shard_map/ppermute | solution.py:27
  191.0 2.7 %multiply_reduce_fusion = (f32[112]{0:T(128)S(1)}, f32[112,3072]{1,0:T(8,128)S(1)}) fusion(bf16[112,3072]{1,0:T(8,128)(2,1)S(1)} %bitcast.70, f32[112]{0:T(128)S(1)} %slice.277, bf16[112,3072]{1,0:T(8,128)(2,1)S(1)} %collective-permute-done.30, bf16[3072,512]{1,0:T(8,128)(2,1)} %bitcast.76, bf16[224,384]{1,0:T(8,128)(2,1)S(1)} %pad_maximum_fusion.9), kind=kOutput, calls=%fused_computation.33 | convolution fusion | flops 266305424 | bytes 5198784 | tf_op jit(solution)/shard_map/dot_general | solution.py:86
  194.2 3.7 %collective-permute-start.32 = (bf16[112,3072]{1,0:T(8,128)(2,1)S(1)}, bf16[112,3072]{1,0:T(8,128)(2,1)S(1)}, u32[]{:S(2)}, u32[]{:S(2)}) collective-permute-start(bf16[112,3072]{1,0:T(8,128)(2,1)S(1)} %fusion.16), channel_id=1, source_target_pairs={{32,0},{64,32},{96,64},{128,96},{160,128},{192,160},{224,192},{33,... | collective-permute-start | bytes 2064392 | tf_op jit(solution)/shard_map/ppermute | solution.py:27
  197.9 2.5 %select_bitcast_fusion.3 = (bf16[1,112,3072]{2,1,0:T(8,128)(2,1)}, bf16[1,112,3072]{2,1,0:T(8,128)(2,1)}) fusion(bf16[224,3072]{1,0:T(8,128)(2,1)} %collective-permute-done.12, pred[]{:T(512)S(6)} %lt.75), kind=kLoop, calls=%fused_computation.46 | loop fusion | flops 688128 | bytes 2752513 | tf_op jit(solution)/shard_map/broadcast_in_dim | solution.py:247
  200.4 2.0 select_bitcast_fusion.5
  202.4 7.0 %collective-permute-done.31 = bf16[112,3072]{1,0:T(8,128)(2,1)S(1)} collective-permute-done((bf16[112,3072]{1,0:T(8,128)(2,1)S(1)}, bf16[112,3072]{1,0:T(8,128)(2,1)S(1)}, u32[]{:S(2)}, u32[]{:S(2)}) %collective-permute-start.31) | collective-permute-done | bytes 688160 | tf_op jit(solution)/shard_map/ppermute | solution.py:27
  209.3 0.8 copy-done.12
  210.2 13.9 %collective-permute-done.32 = bf16[112,3072]{1,0:T(8,128)(2,1)S(1)} collective-permute-done((bf16[112,3072]{1,0:T(8,128)(2,1)S(1)}, bf16[112,3072]{1,0:T(8,128)(2,1)S(1)}, u32[]{:S(2)}, u32[]{:S(2)}) %collective-permute-start.32) | collective-permute-done | bytes 688160 | tf_op jit(solution)/shard_map/ppermute | solution.py:27
  224.1 1.1 convert.33
  225.3 2.3 collective-permute-start.33
  227.6 1.1 collective-permute-start.34
  228.7 1.2 select_bitcast_fusion
  229.8 0.9 select_bitcast_fusion.2
  230.8 2.3 collective-permute-done.35
  (135 shorter events, 11.2 us)
Async XLA Ops:
  7.2 7.3 %copy-start.6 = (bf16[1,112,3072]{2,1,0:T(8,128)(2,1)S(1)}, bf16[1,112,3072]{2,1,0:T(8,128)(2,1)}, u32[]{:S(2)}) copy-start(bf16[1,112,3072]{2,1,0:T(8,128)(2,1)} %param.16) | copy-start | bytes 2064388
  7.2 59.1 %all-gather.3.cloned.1.call-start = ((), (), s32[]{:S(2)}) async-start(), calls=%async_computation.2 | async-start | bytes 3538944 | tf_op jit(solution)/shard_map/all_gather | solution.py:227
  10.4 7.6 %collective-permute-start.4 = (bf16[96,512]{1,0:T(8,128)(2,1)S(1)}, bf16[96,512]{1,0:T(8,128)(2,1)S(1)}, u32[]{:S(2)}, u32[]{:S(2)}) collective-permute-start(bf16[96,512]{1,0:T(8,128)(2,1)S(1)} %get-tuple-element.51), channel_id=1, source_target_pairs={{0,17},{1,16},{16,1},{17,0},{2,19},{3,18},{18,3},{19,2},{4,21},{5,... | collective-permute-start | bytes 294920 | tf_op jit(solution)/shard_map/ppermute | solution.py:210
  12.0 5.9 %collective-permute-start.2 = (bf16[96,512]{1,0:T(8,128)(2,1)S(1)}, bf16[96,512]{1,0:T(8,128)(2,1)S(1)}, u32[]{:S(2)}, u32[]{:S(2)}) collective-permute-start(bf16[96,512]{1,0:T(8,128)(2,1)S(1)} %get-tuple-element.51), channel_id=1, source_target_pairs={{0,1},{1,0},{2,3},{3,2},{4,5},{5,4},{6,7},{7,6},{8,9},{9,8},{10,11... | collective-permute-start | bytes 294920 | tf_op jit(solution)/shard_map/ppermute | solution.py:33
  12.0 5.9 %collective-permute-start.3 = (bf16[96,512]{1,0:T(8,128)(2,1)S(1)}, bf16[96,512]{1,0:T(8,128)(2,1)S(1)}, u32[]{:S(2)}, u32[]{:S(2)}) collective-permute-start(bf16[96,512]{1,0:T(8,128)(2,1)S(1)} %get-tuple-element.50), channel_id=1, source_target_pairs={{0,16},{16,0},{1,17},{17,1},{2,18},{18,2},{3,19},{19,3},{4,20},{20... | collective-permute-start | bytes 294920 | tf_op jit(solution)/shard_map/ppermute | solution.py:33
  14.5 4.4 %copy-start.5 = (bf16[1,112,3072]{2,1,0:T(8,128)(2,1)S(1)}, bf16[1,112,3072]{2,1,0:T(8,128)(2,1)}, u32[]{:S(2)}) copy-start(bf16[1,112,3072]{2,1,0:T(8,128)(2,1)} %param.12) | copy-start | bytes 2064388
  14.5 5.0 %copy-start.15 = (s32[1792]{0:T(1024)S(1)}, s32[1792]{0:T(1024)}, u32[]{:S(2)}) copy-start(s32[1792]{0:T(1024)} %constant.86.clone) | copy-start | bytes 21508
  18.9 205.2 %reduce-scatter.2.cloned.1.call-start = ((), (), s32[]{:S(2)}) async-start(), calls=%async_computation.1 | async-start | bytes 3538944 | tf_op jit(solution)/shard_map/reduce_scatter | solution.py:384
  18.9 8.5 %collective-permute-start.1 = (bf16[112,3072]{1,0:T(8,128)(2,1)S(1)}, bf16[112,3072]{1,0:T(8,128)(2,1)S(1)}, u32[]{:S(2)}, u32[]{:S(2)}) collective-permute-start(bf16[112,3072]{1,0:T(8,128)(2,1)S(1)} %bitcast.83), channel_id=1, source_target_pairs={{0,1},{1,0},{2,3},{3,2},{4,5},{5,4},{6,7},{7,6},{8,9},{9,8},{10,11... | collective-permute-start | bytes 2064392 | tf_op jit(solution)/shard_map/ppermute | solution.py:33
  19.4 8.8 %collective-permute-start = (bf16[224,3072]{1,0:T(8,128)(2,1)}, bf16[224,3072]{1,0:T(8,128)(2,1)S(1)}, u32[]{:S(2)}, u32[]{:S(2)}) collective-permute-start(bf16[224,3072]{1,0:T(8,128)(2,1)} %constant_dynamic-update-slice_fusion), channel_id=1, source_target_pairs={{0,1},{1,0},{2,3},{3,2},{4,5},{5,4},{6,7},{7,6},{8,9},{9,8},{10,11... | collective-permute-start | bytes 4128776 | tf_op jit(solution)/shard_map/ppermute | solution.py:33
  19.7 69.1 %collective-permute-start.12 = (bf16[224,3072]{1,0:T(8,128)(2,1)}, bf16[224,3072]{1,0:T(8,128)(2,1)}, u32[]{:S(2)}, u32[]{:S(2)}) collective-permute-start(bf16[224,3072]{1,0:T(8,128)(2,1)} %constant_dynamic-update-slice_fusion), channel_id=1, source_target_pairs={{32,0},{64,32},{96,64},{128,96},{160,128},{192,160},{224,192},{33,... | collective-permute-start | bytes 4128776 | tf_op jit(solution)/shard_map/ppermute | solution.py:27
  21.7 67.1 %collective-permute-start.11 = (bf16[112,3072]{1,0:T(8,128)(2,1)S(1)}, bf16[112,3072]{1,0:T(8,128)(2,1)}, u32[]{:S(2)}, u32[]{:S(2)}) collective-permute-start(bf16[112,3072]{1,0:T(8,128)(2,1)S(1)} %bitcast.84), channel_id=1, source_target_pairs={{0,32},{32,64},{64,96},{96,128},{128,160},{160,192},{192,224},{1,3... | collective-permute-start | bytes 2064392 | tf_op jit(solution)/shard_map/ppermute | solution.py:27
  28.2 2.4 copy-start.3
  28.2 1.6 copy-start
  66.3 4.5 %copy-start.7 = (bf16[1,112,3072]{2,1,0:T(8,128)(2,1)S(1)}, bf16[1,112,3072]{2,1,0:T(8,128)(2,1)}, u32[]{:S(2)}) copy-start(bf16[1,112,3072]{2,1,0:T(8,128)(2,1)} %param.16) | copy-start | bytes 2064388
  66.3 4.5 %copy-start.8 = (bf16[112,3072]{1,0:T(8,128)(2,1)S(1)}, bf16[112,3072]{1,0:T(8,128)(2,1)}, u32[]{:S(2)}) copy-start(bf16[112,3072]{1,0:T(8,128)(2,1)} %get-tuple-element.95) | copy-start | bytes 2064388
  66.3 11.4 %copy-start.4 = (bf16[448,3072]{1,0:T(8,128)(2,1)S(1)}, bf16[448,3072]{1,0:T(8,128)(2,1)}, u32[]{:S(2)}) copy-start(bf16[448,3072]{1,0:T(8,128)(2,1)} %pad_maximum_fusion) | copy-start | bytes 8257540
  69.2 8.0 %copy-start.1 = (bf16[2,1536,512]{2,1,0:T(8,128)(2,1)S(1)}, bf16[2,1536,512]{2,1,0:T(8,128)(2,1)}, u32[]{:S(2)}) copy-start(bf16[2,1536,512]{2,1,0:T(8,128)(2,1)} %all-gather.3.cloned.1.call-done) | copy-start | bytes 9437188
  69.2 6.3 %collective-permute-start.5 = (bf16[224,512]{1,0:T(8,128)(2,1)S(1)}, bf16[224,512]{1,0:T(8,128)(2,1)S(1)}, u32[]{:S(2)}, u32[]{:S(2)}) collective-permute-start(bf16[224,512]{1,0:T(8,128)(2,1)S(1)} %get-tuple-element.106), channel_id=1, source_target_pairs={{0,14},{2,0},{4,2},{6,4},{8,6},{10,8},{12,10},{14,12},{1,15},{3,1}... | collective-permute-start | bytes 688136 | tf_op jit(solution)/shard_map/ppermute | solution.py:37
  70.5 6.7 %collective-permute-start.6 = (bf16[224,512]{1,0:T(8,128)(2,1)S(1)}, bf16[224,512]{1,0:T(8,128)(2,1)S(1)}, u32[]{:S(2)}, u32[]{:S(2)}) collective-permute-start(bf16[224,512]{1,0:T(8,128)(2,1)S(1)} %get-tuple-element.106), channel_id=1, source_target_pairs={{0,2},{2,4},{4,6},{6,8},{8,10},{10,12},{12,14},{14,0},{1,3},{3,5},... | collective-permute-start | bytes 688136 | tf_op jit(solution)/shard_map/ppermute | solution.py:37
  78.6 21.3 %collective-permute-start.15 = (bf16[224,384]{1,0:T(8,128)(2,1)S(1)}, bf16[224,384]{1,0:T(8,128)(2,1)S(1)}, u32[]{:S(2)}, u32[]{:S(2)}) collective-permute-start(bf16[224,384]{1,0:T(8,128)(2,1)S(1)} %pad_maximum_fusion.8), channel_id=1, source_target_pairs={{16,0},{17,1},{18,2},{19,3},{20,4},{21,5},{22,6},{23,7},{24,8},{25... | collective-permute-start | bytes 516104 | tf_op jit(solution)/shard_map/ppermute | solution.py:252
  79.9 6.2 %collective-permute-start.9 = (bf16[224,512]{1,0:T(8,128)(2,1)S(1)}, bf16[224,512]{1,0:T(8,128)(2,1)S(1)}, u32[]{:S(2)}, u32[]{:S(2)}) collective-permute-start(bf16[224,512]{1,0:T(8,128)(2,1)S(1)} %collective-permute-done.6), channel_id=1, source_target_pairs={{0,2},{2,4},{4,6},{6,8},{8,10},{10,12},{12,14},{14,0},{1,3},{3,5},... | collective-permute-start | bytes 688136 | tf_op jit(solution)/shard_map/ppermute | solution.py:37
  80.0 6.1 %collective-permute-start.7 = (bf16[224,512]{1,0:T(8,128)(2,1)S(1)}, bf16[224,512]{1,0:T(8,128)(2,1)S(1)}, u32[]{:S(2)}, u32[]{:S(2)}) collective-permute-start(bf16[224,512]{1,0:T(8,128)(2,1)S(1)} %collective-permute-done.5), channel_id=1, source_target_pairs={{0,14},{2,0},{4,2},{6,4},{8,6},{10,8},{12,10},{14,12},{1,15},{3,1}... | collective-permute-start | bytes 688136 | tf_op jit(solution)/shard_map/ppermute | solution.py:37
  86.1 6.1 %collective-permute-start.10 = (bf16[224,512]{1,0:T(8,128)(2,1)S(1)}, bf16[224,512]{1,0:T(8,128)(2,1)S(1)}, u32[]{:S(2)}, u32[]{:S(2)}) collective-permute-start(bf16[224,512]{1,0:T(8,128)(2,1)S(1)} %collective-permute-done.9), channel_id=1, source_target_pairs={{0,2},{2,4},{4,6},{6,8},{8,10},{10,12},{12,14},{14,0},{1,3},{3,5},... | collective-permute-start | bytes 688136 | tf_op jit(solution)/shard_map/ppermute | solution.py:37
  86.1 6.1 %collective-permute-start.8 = (bf16[224,512]{1,0:T(8,128)(2,1)S(1)}, bf16[224,512]{1,0:T(8,128)(2,1)S(1)}, u32[]{:S(2)}, u32[]{:S(2)}) collective-permute-start(bf16[224,512]{1,0:T(8,128)(2,1)S(1)} %collective-permute-done.7), channel_id=1, source_target_pairs={{0,14},{2,0},{4,2},{6,4},{8,6},{10,8},{12,10},{14,12},{1,15},{3,1}... | collective-permute-start | bytes 688136 | tf_op jit(solution)/shard_map/ppermute | solution.py:37
  92.2 5.2 %collective-permute-start.13 = (bf16[112,512]{1,0:T(8,128)(2,1)S(1)}, bf16[112,512]{1,0:T(8,128)(2,1)S(1)}, u32[]{:S(2)}, u32[]{:S(2)}) collective-permute-start(bf16[112,512]{1,0:T(8,128)(2,1)S(1)} %slice.245), channel_id=1, source_target_pairs={{0,14},{2,0},{4,2},{6,4},{8,6},{10,8},{12,10},{14,12},{1,15},{3,1}... | collective-permute-start | bytes 344072 | tf_op jit(solution)/shard_map/ppermute | solution.py:37
  94.9 4.9 %collective-permute-start.14 = (bf16[112,512]{1,0:T(8,128)(2,1)S(1)}, bf16[112,512]{1,0:T(8,128)(2,1)S(1)}, u32[]{:S(2)}, u32[]{:S(2)}) collective-permute-start(bf16[112,512]{1,0:T(8,128)(2,1)S(1)} %slice.246), channel_id=1, source_target_pairs={{0,2},{2,4},{4,6},{6,8},{8,10},{10,12},{12,14},{14,0},{1,3},{3,5},... | collective-permute-start | bytes 344072 | tf_op jit(solution)/shard_map/ppermute | solution.py:37
  100.0 9.6 %copy-start.14 = (f32[224,5]{1,0:T(8,128)S(1)}, f32[224,5]{1,0:T(8,128)}, u32[]{:S(2)}) copy-start(f32[224,5]{1,0:T(8,128)} %constant.80.clone.1) | copy-start | bytes 13444
  105.3 4.3 %collective-permute-start.16 = (f32[224,5]{1,0:T(8,128)S(1)}, f32[224,5]{1,0:T(8,128)S(1)}, u32[]{:S(2)}, u32[]{:S(2)}) collective-permute-start(f32[224,5]{1,0:T(8,128)S(1)} %slice_select_fusion), channel_id=1, source_target_pairs={{0,16},{16,0},{1,17},{17,1},{2,18},{18,2},{3,19},{19,3},{4,20},{20... | collective-permute-start | bytes 13448 | tf_op jit(solution)/shard_map/ppermute | solution.py:33
  115.0 6.2 %collective-permute-start.17 = (bf16[112,256]{1,0:T(8,128)(2,1)S(1)}, bf16[112,256]{1,0:T(8,128)(2,1)S(1)}, u32[]{:S(2)}, u32[]{:S(2)}) collective-permute-start(bf16[112,256]{1,0:T(8,128)(2,1)S(1)} %get-tuple-element.100), channel_id=1, source_target_pairs={{0,2},{2,4},{4,6},{6,8},{8,10},{10,12},{12,14},{14,0},{1,3},{3,5},... | collective-permute-start | bytes 172040 | tf_op jit(solution)/shard_map/ppermute | solution.py:37
  115.1 6.1 %collective-permute-start.20 = (bf16[112,256]{1,0:T(8,128)(2,1)S(1)}, bf16[112,256]{1,0:T(8,128)(2,1)S(1)}, u32[]{:S(2)}, u32[]{:S(2)}) collective-permute-start(bf16[112,256]{1,0:T(8,128)(2,1)S(1)} %get-tuple-element.98), channel_id=1, source_target_pairs={{0,14},{2,0},{4,2},{6,4},{8,6},{10,8},{12,10},{14,12},{1,15},{3,1}... | collective-permute-start | bytes 172040 | tf_op jit(solution)/shard_map/ppermute | solution.py:37
  117.8 6.3 %collective-permute-start.23 = (bf16[224,256]{1,0:T(8,128)(2,1)S(1)}, bf16[224,256]{1,0:T(8,128)(2,1)S(1)}, u32[]{:S(2)}, u32[]{:S(2)}) collective-permute-start(bf16[224,256]{1,0:T(8,128)(2,1)S(1)} %slice.432), channel_id=1, source_target_pairs={{0,16},{1,17},{2,18},{3,19},{4,20},{5,21},{6,22},{7,23},{8,24},{9,... | collective-permute-start | bytes 344072 | tf_op jit(solution)/shard_map/ppermute | solution.py:255
  121.3 13.6 %collective-permute-start.18 = (bf16[224,256]{1,0:T(8,128)(2,1)S(1)}, bf16[224,256]{1,0:T(8,128)(2,1)S(1)}, u32[]{:S(2)}, u32[]{:S(2)}) collective-permute-start(bf16[224,256]{1,0:T(8,128)(2,1)S(1)} %pad_maximum_fusion.13), channel_id=1, source_target_pairs={{0,2},{2,4},{4,6},{6,8},{8,10},{10,12},{12,14},{14,0},{1,3},{3,5},... | collective-permute-start | bytes 344072 | tf_op jit(solution)/shard_map/ppermute | solution.py:37
  121.4 18.6 %copy-start.9 = (bf16[1,112,3072]{2,1,0:T(8,128)(2,1)S(1)}, bf16[1,112,3072]{2,1,0:T(8,128)(2,1)}, u32[]{:S(2)}) copy-start(bf16[1,112,3072]{2,1,0:T(8,128)(2,1)} %param.14) | copy-start | bytes 2064388
  121.4 13.5 %collective-permute-start.21 = (bf16[224,256]{1,0:T(8,128)(2,1)S(1)}, bf16[224,256]{1,0:T(8,128)(2,1)S(1)}, u32[]{:S(2)}, u32[]{:S(2)}) collective-permute-start(bf16[224,256]{1,0:T(8,128)(2,1)S(1)} %pad_maximum_fusion.14), channel_id=1, source_target_pairs={{0,14},{2,0},{4,2},{6,4},{8,6},{10,8},{12,10},{14,12},{1,15},{3,1}... | collective-permute-start | bytes 344072 | tf_op jit(solution)/shard_map/ppermute | solution.py:37
  124.5 15.4 %collective-permute-start.24 = (bf16[112,3072]{1,0:T(8,128)(2,1)S(1)}, bf16[112,3072]{1,0:T(8,128)(2,1)S(1)}, u32[]{:S(2)}, u32[]{:S(2)}) collective-permute-start(bf16[112,3072]{1,0:T(8,128)(2,1)S(1)} %convolution_convert_fusion.3), channel_id=1, source_target_pairs={{0,1},{1,0},{2,3},{3,2},{4,5},{5,4},{6,7},{7,6},{8,9},{9,8},{10,11... | collective-permute-start | bytes 2064392 | tf_op jit(solution)/shard_map/ppermute | solution.py:33
  135.0 4.9 %collective-permute-start.19 = (bf16[224,256]{1,0:T(8,128)(2,1)S(1)}, bf16[224,256]{1,0:T(8,128)(2,1)S(1)}, u32[]{:S(2)}, u32[]{:S(2)}) collective-permute-start(bf16[224,256]{1,0:T(8,128)(2,1)S(1)} %get-tuple-element.90), channel_id=1, source_target_pairs={{0,2},{2,4},{4,6},{6,8},{8,10},{10,12},{12,14},{14,0},{1,3},{3,5},... | collective-permute-start | bytes 344072 | tf_op jit(solution)/shard_map/ppermute | solution.py:37
  135.0 4.8 %collective-permute-start.22 = (bf16[224,256]{1,0:T(8,128)(2,1)S(1)}, bf16[224,256]{1,0:T(8,128)(2,1)S(1)}, u32[]{:S(2)}, u32[]{:S(2)}) collective-permute-start(bf16[224,256]{1,0:T(8,128)(2,1)S(1)} %get-tuple-element.89), channel_id=1, source_target_pairs={{0,14},{2,0},{4,2},{6,4},{8,6},{10,8},{12,10},{14,12},{1,15},{3,1}... | collective-permute-start | bytes 344072 | tf_op jit(solution)/shard_map/ppermute | solution.py:37
  140.3 5.2 %collective-permute-start.25 = (bf16[224,256]{1,0:T(8,128)(2,1)S(1)}, bf16[224,256]{1,0:T(8,128)(2,1)S(1)}, u32[]{:S(2)}, u32[]{:S(2)}) collective-permute-start(bf16[224,256]{1,0:T(8,128)(2,1)S(1)} %get-tuple-element.66), channel_id=1, source_target_pairs={{0,2},{2,4},{4,6},{6,8},{8,10},{10,12},{12,14},{14,0},{1,3},{3,5},... | collective-permute-start | bytes 344072 | tf_op jit(solution)/shard_map/ppermute | solution.py:37
  140.7 4.8 %collective-permute-start.26 = (bf16[224,256]{1,0:T(8,128)(2,1)S(1)}, bf16[224,256]{1,0:T(8,128)(2,1)S(1)}, u32[]{:S(2)}, u32[]{:S(2)}) collective-permute-start(bf16[224,256]{1,0:T(8,128)(2,1)S(1)} %get-tuple-element.67), channel_id=1, source_target_pairs={{0,14},{2,0},{4,2},{6,4},{8,6},{10,8},{12,10},{14,12},{1,15},{3,1}... | collective-permute-start | bytes 344072 | tf_op jit(solution)/shard_map/ppermute | solution.py:37
  149.4 14.0 %copy-start.10 = (bf16[1,112,3072]{2,1,0:T(8,128)(2,1)S(1)}, bf16[1,112,3072]{2,1,0:T(8,128)(2,1)}, u32[]{:S(2)}) copy-start(bf16[1,112,3072]{2,1,0:T(8,128)(2,1)} %param.11) | copy-start | bytes 2064388
  149.5 4.3 %collective-permute-start.27 = (bf16[224,128]{1,0:T(8,128)(2,1)S(1)}, bf16[224,128]{1,0:T(8,128)(2,1)S(1)}, u32[]{:S(2)}, u32[]{:S(2)}) collective-permute-start(bf16[224,128]{1,0:T(8,128)(2,1)S(1)} %slice.433), channel_id=1, source_target_pairs={{0,16},{1,17},{2,18},{3,19},{4,20},{5,21},{6,22},{7,23},{8,24},{9,... | collective-permute-start | bytes 172040 | tf_op jit(solution)/shard_map/ppermute | solution.py:255
  155.3 29.7 %copy-start.2 = (bf16[2,1536,512]{2,1,0:T(8,128)(2,1)S(1)}, bf16[2,1536,512]{2,1,0:T(8,128)(2,1)}, u32[]{:S(2)}) copy-start(bf16[2,1536,512]{2,1,0:T(8,128)(2,1)} %all-gather.3.cloned.1.call-done) | copy-start | bytes 9437188
  155.3 8.0 %collective-permute-start.28 = (bf16[112,3072]{1,0:T(8,128)(2,1)S(1)}, bf16[112,3072]{1,0:T(8,128)(2,1)S(1)}, u32[]{:S(2)}, u32[]{:S(2)}) collective-permute-start(bf16[112,3072]{1,0:T(8,128)(2,1)S(1)} %convolution_convert_fusion.2), channel_id=1, source_target_pairs={{0,1},{1,0},{2,3},{3,2},{4,5},{5,4},{6,7},{7,6},{8,9},{9,8},{10,11... | collective-permute-start | bytes 2064392 | tf_op jit(solution)/shard_map/ppermute | solution.py:33
  164.9 20.2 %collective-permute-start.29 = (bf16[112,3072]{1,0:T(8,128)(2,1)S(1)}, bf16[112,3072]{1,0:T(8,128)(2,1)S(1)}, u32[]{:S(2)}, u32[]{:S(2)}) collective-permute-start(bf16[112,3072]{1,0:T(8,128)(2,1)S(1)} %fusion.3), channel_id=1, source_target_pairs={{0,32},{32,64},{64,96},{96,128},{128,160},{160,192},{192,224},{1,3... | collective-permute-start | bytes 2064392 | tf_op jit(solution)/shard_map/ppermute | solution.py:27
  186.8 4.3 %collective-permute-start.30 = (bf16[112,3072]{1,0:T(8,128)(2,1)}, bf16[112,3072]{1,0:T(8,128)(2,1)S(1)}, u32[]{:S(2)}, u32[]{:S(2)}) collective-permute-start(bf16[112,3072]{1,0:T(8,128)(2,1)} %convolution_convert_fusion.1), channel_id=1, source_target_pairs={{0,1},{1,0},{2,3},{3,2},{4,5},{5,4},{6,7},{7,6},{8,9},{9,8},{10,11... | collective-permute-start | bytes 2064392 | tf_op jit(solution)/shard_map/ppermute | solution.py:33
  187.9 5.9 %copy-start.11 = (bf16[1,112,3072]{2,1,0:T(8,128)(2,1)S(1)}, bf16[1,112,3072]{2,1,0:T(8,128)(2,1)}, u32[]{:S(2)}) copy-start(bf16[1,112,3072]{2,1,0:T(8,128)(2,1)} %param.15) | copy-start | bytes 2064388
  187.9 21.5 %collective-permute-start.31 = (bf16[112,3072]{1,0:T(8,128)(2,1)S(1)}, bf16[112,3072]{1,0:T(8,128)(2,1)S(1)}, u32[]{:S(2)}, u32[]{:S(2)}) collective-permute-start(bf16[112,3072]{1,0:T(8,128)(2,1)S(1)} %fusion.2), channel_id=1, source_target_pairs={{32,0},{64,32},{96,64},{128,96},{160,128},{192,160},{224,192},{33,... | collective-permute-start | bytes 2064392 | tf_op jit(solution)/shard_map/ppermute | solution.py:27
  194.2 29.9 %collective-permute-start.32 = (bf16[112,3072]{1,0:T(8,128)(2,1)S(1)}, bf16[112,3072]{1,0:T(8,128)(2,1)S(1)}, u32[]{:S(2)}, u32[]{:S(2)}) collective-permute-start(bf16[112,3072]{1,0:T(8,128)(2,1)S(1)} %fusion.16), channel_id=1, source_target_pairs={{32,0},{64,32},{96,64},{128,96},{160,128},{192,160},{224,192},{33,... | collective-permute-start | bytes 2064392 | tf_op jit(solution)/shard_map/ppermute | solution.py:27
  209.3 0.8 copy-start.12
  224.1 4.6 %copy-start.13 = (bf16[112,3072]{1,0:T(8,128)(2,1)S(1)}, bf16[112,3072]{1,0:T(8,128)(2,1)}, u32[]{:S(2)}) copy-start(bf16[112,3072]{1,0:T(8,128)(2,1)} %copy-done.12) | copy-start | bytes 2064388
  225.3 5.4 %collective-permute-start.33 = (bf16[96,512]{1,0:T(8,128)(2,1)S(1)}, bf16[96,512]{1,0:T(8,128)(2,1)S(1)}, u32[]{:S(2)}, u32[]{:S(2)}) collective-permute-start(bf16[96,512]{1,0:T(8,128)(2,1)S(1)} %get-tuple-element.101), channel_id=1, source_target_pairs={{0,16},{16,0},{1,17},{17,1},{2,18},{18,2},{3,19},{19,3},{4,20},{20... | collective-permute-start | bytes 294920 | tf_op jit(solution)/shard_map/ppermute | solution.py:33
  227.6 3.2 %collective-permute-start.34 = (bf16[96,512]{1,0:T(8,128)(2,1)S(1)}, bf16[96,512]{1,0:T(8,128)(2,1)S(1)}, u32[]{:S(2)}, u32[]{:S(2)}) collective-permute-start(bf16[96,512]{1,0:T(8,128)(2,1)S(1)} %get-tuple-element.103), channel_id=1, source_target_pairs={{0,1},{1,0},{2,3},{3,2},{4,5},{5,4},{6,7},{7,6},{8,9},{9,8},{10,11... | collective-permute-start | bytes 294920 | tf_op jit(solution)/shard_map/ppermute | solution.py:33
  228.7 4.4 %collective-permute-start.35 = (bf16[96,512]{1,0:T(8,128)(2,1)S(1)}, bf16[96,512]{1,0:T(8,128)(2,1)S(1)}, u32[]{:S(2)}, u32[]{:S(2)}) collective-permute-start(bf16[96,512]{1,0:T(8,128)(2,1)S(1)} %get-tuple-element.102), channel_id=1, source_target_pairs={{0,17},{1,16},{16,1},{17,0},{2,19},{3,18},{18,3},{19,2},{4,21},{5,... | collective-permute-start | bytes 294920 | tf_op jit(solution)/shard_map/ppermute | solution.py:415
Sparse Core Ops, SparseCore 0:
  19.0 47.2 all-gather.2
  149.5 48.1 reduce-scatter.1
where the time goes:
time: 243 us; the launch traced here: 242 us
  waiting for transfers between devices  104 us (43%)
  starting transfers between devices  72.5 us (30%)
  other arithmetic  16.1 us (7%)
  between operations  14.8 us (6%)
  matrix products  14.2 us (6%)
  local copies, waits for them, and re-layouts  10.8 us (4%)
  Pallas kernels  9.64 us (4%)
    ppermute x5, waiting for transfers between devices, passed_along(): lax.ppermute(value, 'section', [(source, source + steps) for source in ra...  37.9 us
    all_gather x1, waiting for transfers between devices, per_device(): w_kvqo = lax.all_gather(pair, 'z', axis=1).reshape(-1, 2 * wide)  33.9 us
    ppermute x10, starting transfers between devices, swap(): return lax.ppermute(value, axis, [(0, 1), (1, 0)])  24.3 us
    ppermute x16, waiting for transfers between devices, ring(): return lax.ppermute(value, 'z', [(i, (i + step) % Z) for i in range(Z)])  22 us
    ppermute x16, starting transfers between devices, ring(): return lax.ppermute(value, 'z', [(i, (i + step) % Z) for i in range(Z)])  21.2 us
    ppermute x5, starting transfers between devices, passed_along(): lax.ppermute(value, 'section', [(source, source + steps) for source in ra...  17.6 us
    dot_general x10, matrix products, dot(): lax.dot_general(left, right, (((left_dim,), (right_dim,)), ((), ())), pre...  14.2 us
    pallas_call x2, Pallas kernels, kernel_call(): pl.pallas_call(functools.partial(kernel, chunk), out_shape=[jax.ShapeDtyp...  9.64 us
  transfers between devices with their start and end apart: 38, of which 17 were waited for; matrix products, arithmetic and copies ran while one was open for 11% of the time, Pallas kernels for 0%

commit v1 on v0

--- a/solution.py
+++ b/solution.py
@@ -354,13 +354,12 @@
         {1: (rec_first,)},
     )
     (rec_first,) = beside[1]
-    kv_grad = kv_grad.astype(BF16)
+    kv_grad, next_second = lax.optimization_barrier((kv_grad.astype(BF16), next_second))
     back_first = passed_along(rec_first, -1)
 
     grads = jnp.concatenate([kv_grad, q_grad], axis=1)
-    grads_late, next_second = lax.optimization_barrier((grads, next_second))
-    received = swap(dot(grads_late[tokens:], w_kvq, 1, 1).astype(BF16), "c")
-    normed_grad = dot(grads_late[:tokens], w_kvq, 1, 1) + received.astype(F32)
+    received = swap(dot(grads[tokens:], w_kvq, 1, 1).astype(BF16), "c")
+    normed_grad = dot(grads[:tokens], w_kvq, 1, 1) + received.astype(F32)
     normed_own, inverse_own = stream_b.astype(F32) * inverse_b[:tokens], inverse_b[:tokens]
     input_grad = inverse_own * (
         normed_grad - normed_own * jnp.mean(normed_grad * normed_own, axis=-1, keepdims=True)
@@ -404,19 +403,15 @@
         )
     )
     rows = over_z.shape[0] // (Y * C)
-    corner = over_z.astype(F32).reshape(Y, C, rows, 2 * wide)
-
-    def of(y_, c_):
-        return lax.dynamic_slice(corner, (y_, c_, 0, 0), (1, 1, rows, 2 * wide))[0, 0]
-
-    def of_other(c_):
-        return of(1 - y, c_).astype(BF16)
-
-    across = lax.ppermute(
-        of_other(1 - c), ("yl", "c"), [(i, Y * C - 1 - i) for i in range(Y * C)]
-    ).astype(F32)
-    own = of(y, c) + swap(of_other(c), "yl").astype(F32)
-    other = swap(of(y, 1 - c).astype(BF16), "c").astype(F32) + across
+    by_owner = over_z.reshape(Y, C, rows, 2 * wide)
+
+    def of_core(core):
+        return lax.dynamic_slice(by_owner, (0, core, 0, 0), (Y, 1, rows, 2 * wide))[:, 0]
+
+    both = jnp.concatenate([of_core(c), swap(of_core(1 - c), "c")], axis=2)
+    kept = jnp.where(y == 0, both[0], both[1]).astype(F32)
+    whole = kept + swap(jnp.where(y == 0, both[1], both[0]), "yl").astype(F32)
+    own, other = whole[:, : 2 * wide], whole[:, 2 * wide :]
 
     def heads_of(index):
         span = slice(index * HEAD_DIM, (index + 1) * HEAD_DIM)

time: 243 us -> 237 us (0.975)
  waiting for transfers between devices: 104 us -> 97.5 us
  other arithmetic: 16.1 us -> 19.6 us
    ppermute x5, waiting for transfers between devices: 37.9 us -> 27.7 us  [passed_along(): lax.ppermute(value, 'section', [(source, source + steps) for source in ra...]
    reduce_scatter x1, waiting for transfers between devices: 0.01 us -> 5.16 us  [per_device(): lax.psum_scatter(by_chip.reshape(-1, 2 * wide), 'z', scatter_dimension=0,...]
    ppermute x10, waiting for transfers between devices: 6.47 us -> 11 us  [swap(): return lax.ppermute(value, axis, [(0, 1), (1, 0)])]
  transfers between devices with their start and end apart: 38 -> 37, of which waited for: 17 -> 16; matrix products, arithmetic and copies ran while one was open for 11% -> 12% of each run, Pallas kernels for 0% -> 2%
where the time goes in v1:
time: 237 us; the launch traced here: 235 us
  waiting for transfers between devices  97.5 us (41%)
  starting transfers between devices  71.5 us (30%)
  other arithmetic  19.6 us (8%)
  between operations  14.8 us (6%)
  matrix products  12.4 us (5%)
  local copies, waits for them, and re-layouts  9.95 us (4%)
  Pallas kernels  9.63 us (4%)
    all_gather x1, waiting for transfers between devices, per_device(): w_kvqo = lax.all_gather(pair, 'z', axis=1).reshape(-1, 2 * wide)  31.6 us
    ppermute x5, waiting for transfers between devices, passed_along(): lax.ppermute(value, 'section', [(source, source + steps) for source in ra...  27.7 us
    ppermute x10, starting transfers between devices, swap(): return lax.ppermute(value, axis, [(0, 1), (1, 0)])  25.2 us
    ppermute x16, waiting for transfers between devices, ring(): return lax.ppermute(value, 'z', [(i, (i + step) % Z) for i in range(Z)])  22.1 us
    ppermute x16, starting transfers between devices, ring(): return lax.ppermute(value, 'z', [(i, (i + step) % Z) for i in range(Z)])  20.8 us
    ppermute x5, starting transfers between devices, passed_along(): lax.ppermute(value, 'section', [(source, source + steps) for source in ra...  17.8 us
    dot_general x10, matrix products, dot(): lax.dot_general(left, right, (((left_dim,), (right_dim,)), ((), ())), pre...  12.4 us
    ppermute x10, waiting for transfers between devices, swap(): return lax.ppermute(value, axis, [(0, 1), (1, 0)])  11 us
  transfers between devices with their start and end apart: 37, of which 16 were waited for; matrix products, arithmetic and copies ran while one was open for 12% of the time, Pallas kernels for 2%

profile of v1, /device:TPU:19, one launch (start us, length us, event | category | flops | bytes accessed | tf_op | source)
XLA Modules:
  0.0 235.4 jit_solution(14777655547740525744)
XLA Ops:
  7.2 0.8 fusion.83
  9.6 0.8 fusion.86
  10.4 1.6 collective-permute-start.4
  12.5 1.1 constant_dynamic-update-slice_fusion.1
  13.7 4.2 %collective-permute-done.3 = bf16[96,512]{1,0:T(8,128)(2,1)S(1)} collective-permute-done((bf16[96,512]{1,0:T(8,128)(2,1)S(1)}, bf16[96,512]{1,0:T(8,128)(2,1)S(1)}, u32[]{:S(2)}, u32[]{:S(2)}) %collective-permute-start.3) | collective-permute-done | bytes 98336 | tf_op jit(solution)/shard_map/ppermute | solution.py:33
  18.0 0.8 maximum_select_fusion
  19.7 2.0 collective-permute-start.12
  21.7 5.7 %collective-permute-start.11 = (bf16[112,3072]{1,0:T(8,128)(2,1)}, bf16[112,3072]{1,0:T(8,128)(2,1)}, u32[]{:S(2)}, u32[]{:S(2)}) collective-permute-start(bf16[112,3072]{1,0:T(8,128)(2,1)} %bitcast.6), channel_id=1, source_target_pairs={{0,32},{32,64},{64,96},{96,128},{128,160},{160,192},{192,224},{1,3... | collective-permute-start | bytes 2064392 | tf_op jit(solution)/shard_map/ppermute | solution.py:27
  27.4 1.5 fusion.8
  28.9 1.5 fusion.9
  30.5 0.9 fusion.76
  32.8 1.9 pad_maximum_fusion
  34.7 31.6 %all-gather.3.cloned.1.call-done = bf16[2,1536,512]{2,1,0:T(8,128)(2,1)} async-done(((bf16[2,192,512]{2,1,0:T(8,128)(2,1)}), bf16[2,1536,512]{2,1,0:T(8,128)(2,1)}) %all-gather.3.cloned.1.call-update) | async-done | bytes 3145744 | tf_op jit(solution)/shard_map/all_gather | solution.py:227
  66.3 2.8 %fusion.18 = bf16[448,256]{1,0:T(8,128)(2,1)S(1)} fusion(bf16[3072,512]{1,0:T(8,128)(2,1)} %bitcast.67, bf16[224,3072]{1,0:T(8,128)(2,1)S(1)} %fusion.7, bf16[224,3072]{1,0:T(8,128)(2,1)} %copy-done.5), kind=kOutput, calls=%fused_computation.36 | convolution fusion | flops 710262784 | bytes 4554752 | tf_op jit(solution)/shard_map/dot_general | solution.py:86
  69.2 1.2 collective-permute-start.5
  70.9 4.6 %collective-permute-done.5 = bf16[224,512]{1,0:T(8,128)(2,1)S(1)} collective-permute-done((bf16[224,512]{1,0:T(8,128)(2,1)S(1)}, bf16[224,512]{1,0:T(8,128)(2,1)S(1)}, u32[]{:S(2)}, u32[]{:S(2)}) %collective-permute-start.5) | collective-permute-done | bytes 229408 | tf_op jit(solution)/shard_map/ppermute | solution.py:37
  75.5 1.6 collective-permute-done.6
  77.7 0.9 convolution_convert_fusion.4
  78.6 1.3 collective-permute-start.15
  80.0 2.7 %collective-permute-start.7 = (bf16[224,512]{1,0:T(8,128)(2,1)S(1)}, bf16[224,512]{1,0:T(8,128)(2,1)S(1)}, u32[]{:S(2)}, u32[]{:S(2)}) collective-permute-start(bf16[224,512]{1,0:T(8,128)(2,1)S(1)} %collective-permute-done.5), channel_id=1, source_target_pairs={{0,14},{2,0},{4,2},{6,4},{8,6},{10,8},{12,10},{14,12},{1,15},{3,1}... | collective-permute-start | bytes 688136 | tf_op jit(solution)/shard_map/ppermute | solution.py:37
  82.7 3.4 %collective-permute-done.9 = bf16[224,512]{1,0:T(8,128)(2,1)S(1)} collective-permute-done((bf16[224,512]{1,0:T(8,128)(2,1)S(1)}, bf16[224,512]{1,0:T(8,128)(2,1)S(1)}, u32[]{:S(2)}, u32[]{:S(2)}) %collective-permute-start.9) | collective-permute-done | bytes 229408 | tf_op jit(solution)/shard_map/ppermute | solution.py:37
  86.1 2.7 %collective-permute-start.8 = (bf16[224,512]{1,0:T(8,128)(2,1)S(1)}, bf16[224,512]{1,0:T(8,128)(2,1)S(1)}, u32[]{:S(2)}, u32[]{:S(2)}) collective-permute-start(bf16[224,512]{1,0:T(8,128)(2,1)S(1)} %collective-permute-done.7), channel_id=1, source_target_pairs={{0,14},{2,0},{4,2},{6,4},{8,6},{10,8},{12,10},{14,12},{1,15},{3,1}... | collective-permute-start | bytes 688136 | tf_op jit(solution)/shard_map/ppermute | solution.py:37
  88.8 3.3 %collective-permute-done.10 = bf16[224,512]{1,0:T(8,128)(2,1)S(1)} collective-permute-done((bf16[224,512]{1,0:T(8,128)(2,1)S(1)}, bf16[224,512]{1,0:T(8,128)(2,1)S(1)}, u32[]{:S(2)}, u32[]{:S(2)}) %collective-permute-start.10) | collective-permute-done | bytes 229408 | tf_op jit(solution)/shard_map/ppermute | solution.py:37
  92.2 2.8 %collective-permute-start.13 = (bf16[112,512]{1,0:T(8,128)(2,1)S(1)}, bf16[112,512]{1,0:T(8,128)(2,1)S(1)}, u32[]{:S(2)}, u32[]{:S(2)}) collective-permute-start(bf16[112,512]{1,0:T(8,128)(2,1)S(1)} %slice.263), channel_id=1, source_target_pairs={{0,14},{2,0},{4,2},{6,4},{8,6},{10,8},{12,10},{14,12},{1,15},{3,1}... | collective-permute-start | bytes 344072 | tf_op jit(solution)/shard_map/ppermute | solution.py:37
  95.1 2.3 collective-permute-done.13
  97.4 2.5 %collective-permute-done.14 = bf16[112,512]{1,0:T(8,128)(2,1)S(1)} collective-permute-done((bf16[112,512]{1,0:T(8,128)(2,1)S(1)}, bf16[112,512]{1,0:T(8,128)(2,1)S(1)}, u32[]{:S(2)}, u32[]{:S(2)}) %collective-permute-start.14) | collective-permute-done | bytes 114720 | tf_op jit(solution)/shard_map/ppermute | solution.py:37
  100.0 5.2 %shard_map.186 = (f32[448,8]{1,0:T(8,128)S(1)}, f32[448,128]{1,0:T(8,128)S(1)}) custom-call(bf16[448,128]{1,0:T(8,128)(2,1)S(1)} %pad_maximum_fusion.10.q_b, bf16[448,128]{1,0:T(8,128)(2,1)S(1)} %pad_maximum_fusion.11.g_b, bf16[448,128]{1,0:T(8,128)(2,1)S(1)} %pad_maximum_fusion.12.q_f, bf16[1792,512]{1,0:T(8,128)(2,1)S(1)} %constant_dynamic-update-slice_fusion.2.kv, ...), custom_call_target="tpu_custom_call" | custom-call | flops 822083584 | bytes 2188032 | tf_op jit(solution)/shard_map/pallas_call | solution.py:144
  105.3 2.2 collective-permute-start.16
  107.4 2.2 collective-permute-done.16
  110.4 3.4 %collective-permute-start.27 = (bf16[224,128]{1,0:T(8,128)(2,1)S(1)}, bf16[224,128]{1,0:T(8,128)(2,1)S(1)}, u32[]{:S(2)}, u32[]{:S(2)}) collective-permute-start(bf16[224,128]{1,0:T(8,128)(2,1)S(1)} %slice.475), channel_id=1, source_target_pairs={{0,16},{1,17},{2,18},{3,19},{4,20},{5,21},{6,22},{7,23},{8,24},{9,... | collective-permute-start | bytes 172040 | tf_op jit(solution)/shard_map/ppermute | solution.py:255
  114.0 4.4 %shard_map.187 = (f32[448,256]{1,0:T(8,128)S(1)}, f32[1792,256]{1,0:T(8,128)S(1)}) custom-call(bf16[448,128]{1,0:T(8,128)(2,1)S(1)} %pad_maximum_fusion.10.q_b, bf16[448,128]{1,0:T(8,128)(2,1)S(1)} %pad_maximum_fusion.11.g_b, bf16[1792,512]{1,0:T(8,128)(2,1)S(1)} %constant_dynamic-update-slice_fusion.2.kv, s32[448,1]{1,0:T(8,128)S(1)} %select_add_fusion.query_at, ...), custom_call_target="tpu_custom_call" | custom-call | flops 1233125376 | bytes 2078720 | tf_op jit(solution)/shard_map/pallas_call | solution.py:144
  118.5 1.3 collective-permute-start.23
  120.0 2.7 %collective-permute-start.20 = (bf16[112,256]{1,0:T(8,128)(2,1)S(1)}, bf16[112,256]{1,0:T(8,128)(2,1)S(1)}, u32[]{:S(2)}, u32[]{:S(2)}) collective-permute-start(bf16[112,256]{1,0:T(8,128)(2,1)S(1)} %get-tuple-element.98), channel_id=1, source_target_pairs={{0,14},{2,0},{4,2},{6,4},{8,6},{10,8},{12,10},{14,12},{1,15},{3,1}... | collective-permute-start | bytes 172040 | tf_op jit(solution)/shard_map/ppermute | solution.py:37
  123.0 9.9 %collective-permute-start.28 = (bf16[112,3072]{1,0:T(8,128)(2,1)S(1)}, bf16[112,3072]{1,0:T(8,128)(2,1)S(1)}, u32[]{:S(2)}, u32[]{:S(2)}) collective-permute-start(bf16[112,3072]{1,0:T(8,128)(2,1)S(1)} %convolution_convert_fusion.2), channel_id=1, source_target_pairs={{0,1},{1,0},{2,3},{3,2},{4,5},{5,4},{6,7},{7,6},{8,9},{9,8},{10,11... | collective-permute-start | bytes 2064392 | tf_op jit(solution)/shard_map/ppermute | solution.py:33
  133.1 2.7 %collective-permute-start.21 = (bf16[224,256]{1,0:T(8,128)(2,1)S(1)}, bf16[224,256]{1,0:T(8,128)(2,1)S(1)}, u32[]{:S(2)}, u32[]{:S(2)}) collective-permute-start(bf16[224,256]{1,0:T(8,128)(2,1)S(1)} %pad_maximum_fusion.14), channel_id=1, source_target_pairs={{0,14},{2,0},{4,2},{6,4},{8,6},{10,8},{12,10},{14,12},{1,15},{3,1}... | collective-permute-start | bytes 344072 | tf_op jit(solution)/shard_map/ppermute | solution.py:37
  136.2 2.3 collective-permute-start.24
  138.7 2.7 %collective-permute-start.22 = (bf16[224,256]{1,0:T(8,128)(2,1)S(1)}, bf16[224,256]{1,0:T(8,128)(2,1)S(1)}, u32[]{:S(2)}, u32[]{:S(2)}) collective-permute-start(bf16[224,256]{1,0:T(8,128)(2,1)S(1)} %get-tuple-element.89), channel_id=1, source_target_pairs={{0,14},{2,0},{4,2},{6,4},{8,6},{10,8},{12,10},{14,12},{1,15},{3,1}... | collective-permute-start | bytes 344072 | tf_op jit(solution)/shard_map/ppermute | solution.py:37
  141.4 2.2 collective-permute-done.19
  144.0 3.2 %collective-permute-start.29 = (bf16[112,3072]{1,0:T(8,128)(2,1)S(1)}, bf16[112,3072]{1,0:T(8,128)(2,1)S(1)}, u32[]{:S(2)}, u32[]{:S(2)}) collective-permute-start(bf16[112,3072]{1,0:T(8,128)(2,1)S(1)} %fusion.3), channel_id=1, source_target_pairs={{0,32},{32,64},{64,96},{96,128},{128,160},{160,192},{192,224},{1,3... | collective-permute-start | bytes 2064392 | tf_op jit(solution)/shard_map/ppermute | solution.py:27
  147.2 1.2 fusion.2
  148.5 1.2 collective-permute-start.25
  149.6 1.5 collective-permute-start.26
  151.2 2.2 collective-permute-done.25
  153.4 6.6 %collective-permute-done.29 = bf16[112,3072]{1,0:T(8,128)(2,1)S(1)} collective-permute-done((bf16[112,3072]{1,0:T(8,128)(2,1)S(1)}, bf16[112,3072]{1,0:T(8,128)(2,1)S(1)}, u32[]{:S(2)}, u32[]{:S(2)}) %collective-permute-start.29) | collective-permute-done | bytes 688160 | tf_op jit(solution)/shard_map/ppermute | solution.py:27
  160.0 0.8 copy-done.12
  160.9 1.9 convolution_convert_fusion
  162.7 1.8 copy.40
  164.6 1.7 convolution_convert_fusion.1
  166.3 5.4 %collective-permute-start.30 = (bf16[112,3072]{1,0:T(8,128)(2,1)}, bf16[112,3072]{1,0:T(8,128)(2,1)}, u32[]{:S(2)}, u32[]{:S(2)}) collective-permute-start(bf16[112,3072]{1,0:T(8,128)(2,1)} %convolution_convert_fusion.1), channel_id=1, source_target_pairs={{0,1},{1,0},{2,3},{3,2},{4,5},{5,4},{6,7},{7,6},{8,9},{9,8},{10,11... | collective-permute-start | bytes 2064392 | tf_op jit(solution)/shard_map/ppermute | solution.py:33
  171.7 3.2 %collective-permute-start.31 = (bf16[112,3072]{1,0:T(8,128)(2,1)}, bf16[112,3072]{1,0:T(8,128)(2,1)}, u32[]{:S(2)}, u32[]{:S(2)}) collective-permute-start(bf16[112,3072]{1,0:T(8,128)(2,1)} %fusion.2), channel_id=1, source_target_pairs={{32,0},{64,32},{96,64},{128,96},{160,128},{192,160},{224,192},{33,... | collective-permute-start | bytes 2064392 | tf_op jit(solution)/shard_map/ppermute | solution.py:27
  174.9 2.3 multiply_reduce_fusion
  177.2 1.6 fusion.17
  178.8 3.7 %collective-permute-start.32 = (bf16[112,3072]{1,0:T(8,128)(2,1)S(1)}, bf16[112,3072]{1,0:T(8,128)(2,1)S(1)}, u32[]{:S(2)}, u32[]{:S(2)}) collective-permute-start(bf16[112,3072]{1,0:T(8,128)(2,1)S(1)} %fusion.17), channel_id=1, source_target_pairs={{32,0},{64,32},{96,64},{128,96},{160,128},{192,160},{224,192},{33,... | collective-permute-start | bytes 2064392 | tf_op jit(solution)/shard_map/ppermute | solution.py:27
  182.6 2.5 %select_bitcast_fusion.3 = (bf16[1,112,3072]{2,1,0:T(8,128)(2,1)}, bf16[1,112,3072]{2,1,0:T(8,128)(2,1)}) fusion(bf16[224,3072]{1,0:T(8,128)(2,1)} %collective-permute-done.12, pred[]{:T(512)S(6)} %lt.65), kind=kLoop, calls=%fused_computation.47 | loop fusion | flops 688128 | bytes 2752513 | tf_op jit(solution)/shard_map/broadcast_in_dim | solution.py:247
  185.0 2.0 select_bitcast_fusion.5
  187.0 6.4 %collective-permute-done.31 = bf16[112,3072]{1,0:T(8,128)(2,1)} collective-permute-done((bf16[112,3072]{1,0:T(8,128)(2,1)}, bf16[112,3072]{1,0:T(8,128)(2,1)}, u32[]{:S(2)}, u32[]{:S(2)}) %collective-permute-start.31) | collective-permute-done | bytes 688160 | tf_op jit(solution)/shard_map/ppermute | solution.py:27
  193.5 14.6 %collective-permute-done.32 = bf16[112,3072]{1,0:T(8,128)(2,1)S(1)} collective-permute-done((bf16[112,3072]{1,0:T(8,128)(2,1)S(1)}, bf16[112,3072]{1,0:T(8,128)(2,1)S(1)}, u32[]{:S(2)}, u32[]{:S(2)}) %collective-permute-start.32) | collective-permute-done | bytes 688160 | tf_op jit(solution)/shard_map/ppermute | solution.py:27
  208.1 5.2 %reduce-scatter.2.cloned.1.call-done = bf16[384,512]{1,0:T(8,128)(2,1)} async-done(((bf16[3072,512]{1,0:T(8,128)(2,1)}), bf16[384,512]{1,0:T(8,128)(2,1)}) %reduce-scatter.2.cloned.1.call-update) | async-done | bytes 393232 | tf_op jit(solution)/shard_map/reduce_scatter | solution.py:383
  213.3 1.0 dynamic-slice_bitcast_fusion.1
  214.3 3.3 %collective-permute-start.33 = (bf16[2,96,512]{2,1,0:T(8,128)(2,1)S(1)}, bf16[2,96,512]{2,1,0:T(8,128)(2,1)S(1)}, u32[]{:S(2)}, u32[]{:S(2)}) collective-permute-start(bf16[2,96,512]{2,1,0:T(8,128)(2,1)S(1)} %get-tuple-element.111), channel_id=1, source_target_pairs={{0,1},{1,0},{2,3},{3,2},{4,5},{5,4},{6,7},{7,6},{8,9},{9,8},{10,11... | collective-permute-start | bytes 589832 | tf_op jit(solution)/shard_map/ppermute | solution.py:33
  217.6 2.3 select_bitcast_fusion
  219.9 1.1 collective-permute-start.34
  221.0 0.9 select_bitcast_fusion.2
  221.9 4.6 %collective-permute-done.34 = bf16[96,1024]{1,0:T(8,128)(2,1)S(1)} collective-permute-done((bf16[96,1024]{1,0:T(8,128)(2,1)S(1)}, bf16[96,1024]{1,0:T(8,128)(2,1)S(1)}, u32[]{:S(2)}, u32[]{:S(2)}) %collective-permute-start.34) | collective-permute-done | bytes 196640 | tf_op jit(solution)/shard_map/ppermute | solution.py:33
  (134 shorter events, 10.8 us)
Async XLA Ops:
  7.2 6.5 %copy-start.7 = (bf16[1,112,3072]{2,1,0:T(8,128)(2,1)S(1)}, bf16[1,112,3072]{2,1,0:T(8,128)(2,1)}, u32[]{:S(2)}) copy-start(bf16[1,112,3072]{2,1,0:T(8,128)(2,1)} %param.16) | copy-start | bytes 2064388
  7.2 59.1 %all-gather.3.cloned.1.call-start = ((), (), s32[]{:S(2)}) async-start(), calls=%async_computation.2 | async-start | bytes 3538944 | tf_op jit(solution)/shard_map/all_gather | solution.py:227
  10.4 7.6 %collective-permute-start.4 = (bf16[96,512]{1,0:T(8,128)(2,1)S(1)}, bf16[96,512]{1,0:T(8,128)(2,1)S(1)}, u32[]{:S(2)}, u32[]{:S(2)}) collective-permute-start(bf16[96,512]{1,0:T(8,128)(2,1)S(1)} %get-tuple-element.51), channel_id=1, source_target_pairs={{0,17},{1,16},{16,1},{17,0},{2,19},{3,18},{18,3},{19,2},{4,21},{5,... | collective-permute-start | bytes 294920 | tf_op jit(solution)/shard_map/ppermute | solution.py:210
  12.0 5.9 %collective-permute-start.2 = (bf16[96,512]{1,0:T(8,128)(2,1)S(1)}, bf16[96,512]{1,0:T(8,128)(2,1)S(1)}, u32[]{:S(2)}, u32[]{:S(2)}) collective-permute-start(bf16[96,512]{1,0:T(8,128)(2,1)S(1)} %get-tuple-element.51), channel_id=1, source_target_pairs={{0,1},{1,0},{2,3},{3,2},{4,5},{5,4},{6,7},{7,6},{8,9},{9,8},{10,11... | collective-permute-start | bytes 294920 | tf_op jit(solution)/shard_map/ppermute | solution.py:33
  12.0 5.9 %collective-permute-start.3 = (bf16[96,512]{1,0:T(8,128)(2,1)S(1)}, bf16[96,512]{1,0:T(8,128)(2,1)S(1)}, u32[]{:S(2)}, u32[]{:S(2)}) collective-permute-start(bf16[96,512]{1,0:T(8,128)(2,1)S(1)} %get-tuple-element.50), channel_id=1, source_target_pairs={{0,16},{16,0},{1,17},{17,1},{2,18},{18,2},{3,19},{19,3},{4,20},{20... | collective-permute-start | bytes 294920 | tf_op jit(solution)/shard_map/ppermute | solution.py:33
  13.7 5.9 %copy-start.17 = (s32[1792]{0:T(1024)S(1)}, s32[1792]{0:T(1024)}, u32[]{:S(2)}) copy-start(s32[1792]{0:T(1024)} %constant.85.clone) | copy-start | bytes 21508
  13.7 5.1 %copy-start.15 = (bf16[224,3072]{1,0:T(8,128)(2,1)}, bf16[224,3072]{1,0:T(8,128)(2,1)S(1)}, u32[]{:S(2)}) copy-start(bf16[224,3072]{1,0:T(8,128)(2,1)S(1)} %constant_dynamic-update-slice_fusion) | copy-start | bytes 4128772
  18.9 194.4 %reduce-scatter.2.cloned.1.call-start = ((), (), s32[]{:S(2)}) async-start(), calls=%async_computation.1 | async-start | bytes 3538944 | tf_op jit(solution)/shard_map/reduce_scatter | solution.py:383
  18.9 8.5 %collective-permute-start.1 = (bf16[112,3072]{1,0:T(8,128)(2,1)}, bf16[112,3072]{1,0:T(8,128)(2,1)S(1)}, u32[]{:S(2)}, u32[]{:S(2)}) collective-permute-start(bf16[112,3072]{1,0:T(8,128)(2,1)} %bitcast.6), channel_id=1, source_target_pairs={{0,1},{1,0},{2,3},{3,2},{4,5},{5,4},{6,7},{7,6},{8,9},{9,8},{10,11... | collective-permute-start | bytes 2064392 | tf_op jit(solution)/shard_map/ppermute | solution.py:33
  19.4 11.1 %collective-permute-start = (bf16[224,3072]{1,0:T(8,128)(2,1)}, bf16[224,3072]{1,0:T(8,128)(2,1)S(1)}, u32[]{:S(2)}, u32[]{:S(2)}) collective-permute-start(bf16[224,3072]{1,0:T(8,128)(2,1)} %copy-done.15), channel_id=1, source_target_pairs={{0,1},{1,0},{2,3},{3,2},{4,5},{5,4},{6,7},{7,6},{8,9},{9,8},{10,11... | collective-permute-start | bytes 4128776 | tf_op jit(solution)/shard_map/ppermute | solution.py:33
  19.7 69.1 %collective-permute-start.12 = (bf16[224,3072]{1,0:T(8,128)(2,1)}, bf16[224,3072]{1,0:T(8,128)(2,1)}, u32[]{:S(2)}, u32[]{:S(2)}) collective-permute-start(bf16[224,3072]{1,0:T(8,128)(2,1)} %copy-done.15), channel_id=1, source_target_pairs={{32,0},{64,32},{96,64},{128,96},{160,128},{192,160},{224,192},{33,... | collective-permute-start | bytes 4128776 | tf_op jit(solution)/shard_map/ppermute | solution.py:27
  21.7 67.1 %collective-permute-start.11 = (bf16[112,3072]{1,0:T(8,128)(2,1)}, bf16[112,3072]{1,0:T(8,128)(2,1)}, u32[]{:S(2)}, u32[]{:S(2)}) collective-permute-start(bf16[112,3072]{1,0:T(8,128)(2,1)} %bitcast.6), channel_id=1, source_target_pairs={{0,32},{32,64},{64,96},{96,128},{128,160},{160,192},{192,224},{1,3... | collective-permute-start | bytes 2064392 | tf_op jit(solution)/shard_map/ppermute | solution.py:27
  30.4 2.4 %copy-start.5 = (bf16[224,3072]{1,0:T(8,128)(2,1)}, bf16[224,3072]{1,0:T(8,128)(2,1)S(1)}, u32[]{:S(2)}) copy-start(bf16[224,3072]{1,0:T(8,128)(2,1)S(1)} %fusion.9) | copy-start | bytes 4128772
  30.4 1.6 copy-start.1
  32.8 33.5 %copy-start.3 = (bf16[224,3072]{1,0:T(8,128)(2,1)}, bf16[224,3072]{1,0:T(8,128)(2,1)S(1)}, u32[]{:S(2)}) copy-start(bf16[224,3072]{1,0:T(8,128)(2,1)S(1)} %fusion.7) | copy-start | bytes 4128772
  66.3 4.5 %copy-start.8 = (bf16[1,112,3072]{2,1,0:T(8,128)(2,1)S(1)}, bf16[1,112,3072]{2,1,0:T(8,128)(2,1)}, u32[]{:S(2)}) copy-start(bf16[1,112,3072]{2,1,0:T(8,128)(2,1)} %param.16) | copy-start | bytes 2064388
  66.3 4.5 %copy-start.9 = (bf16[112,3072]{1,0:T(8,128)(2,1)S(1)}, bf16[112,3072]{1,0:T(8,128)(2,1)}, u32[]{:S(2)}) copy-start(bf16[112,3072]{1,0:T(8,128)(2,1)} %get-tuple-element.95) | copy-start | bytes 2064388
  66.3 11.4 %copy-start.6 = (bf16[448,3072]{1,0:T(8,128)(2,1)S(1)}, bf16[448,3072]{1,0:T(8,128)(2,1)}, u32[]{:S(2)}) copy-start(bf16[448,3072]{1,0:T(8,128)(2,1)} %pad_maximum_fusion) | copy-start | bytes 8257540
  69.2 8.0 %copy-start = (bf16[2,1536,512]{2,1,0:T(8,128)(2,1)S(1)}, bf16[2,1536,512]{2,1,0:T(8,128)(2,1)}, u32[]{:S(2)}) copy-start(bf16[2,1536,512]{2,1,0:T(8,128)(2,1)} %all-gather.3.cloned.1.call-done) | copy-start | bytes 9437188
  69.2 6.3 %collective-permute-start.5 = (bf16[224,512]{1,0:T(8,128)(2,1)S(1)}, bf16[224,512]{1,0:T(8,128)(2,1)S(1)}, u32[]{:S(2)}, u32[]{:S(2)}) collective-permute-start(bf16[224,512]{1,0:T(8,128)(2,1)S(1)} %get-tuple-element.113), channel_id=1, source_target_pairs={{0,14},{2,0},{4,2},{6,4},{8,6},{10,8},{12,10},{14,12},{1,15},{3,1}... | collective-permute-start | bytes 688136 | tf_op jit(solution)/shard_map/ppermute | solution.py:37
  70.5 6.7 %collective-permute-start.6 = (bf16[224,512]{1,0:T(8,128)(2,1)S(1)}, bf16[224,512]{1,0:T(8,128)(2,1)S(1)}, u32[]{:S(2)}, u32[]{:S(2)}) collective-permute-start(bf16[224,512]{1,0:T(8,128)(2,1)S(1)} %get-tuple-element.113), channel_id=1, source_target_pairs={{0,2},{2,4},{4,6},{6,8},{8,10},{10,12},{12,14},{14,0},{1,3},{3,5},... | collective-permute-start | bytes 688136 | tf_op jit(solution)/shard_map/ppermute | solution.py:37
  78.6 21.3 %collective-permute-start.15 = (bf16[224,384]{1,0:T(8,128)(2,1)S(1)}, bf16[224,384]{1,0:T(8,128)(2,1)S(1)}, u32[]{:S(2)}, u32[]{:S(2)}) collective-permute-start(bf16[224,384]{1,0:T(8,128)(2,1)S(1)} %pad_maximum_fusion.9), channel_id=1, source_target_pairs={{16,0},{17,1},{18,2},{19,3},{20,4},{21,5},{22,6},{23,7},{24,8},{25... | collective-permute-start | bytes 516104 | tf_op jit(solution)/shard_map/ppermute | solution.py:252
  79.9 6.2 %collective-permute-start.9 = (bf16[224,512]{1,0:T(8,128)(2,1)S(1)}, bf16[224,512]{1,0:T(8,128)(2,1)S(1)}, u32[]{:S(2)}, u32[]{:S(2)}) collective-permute-start(bf16[224,512]{1,0:T(8,128)(2,1)S(1)} %collective-permute-done.6), channel_id=1, source_target_pairs={{0,2},{2,4},{4,6},{6,8},{8,10},{10,12},{12,14},{14,0},{1,3},{3,5},... | collective-permute-start | bytes 688136 | tf_op jit(solution)/shard_map/ppermute | solution.py:37
  80.0 6.1 %collective-permute-start.7 = (bf16[224,512]{1,0:T(8,128)(2,1)S(1)}, bf16[224,512]{1,0:T(8,128)(2,1)S(1)}, u32[]{:S(2)}, u32[]{:S(2)}) collective-permute-start(bf16[224,512]{1,0:T(8,128)(2,1)S(1)} %collective-permute-done.5), channel_id=1, source_target_pairs={{0,14},{2,0},{4,2},{6,4},{8,6},{10,8},{12,10},{14,12},{1,15},{3,1}... | collective-permute-start | bytes 688136 | tf_op jit(solution)/shard_map/ppermute | solution.py:37
  86.1 6.1 %collective-permute-start.10 = (bf16[224,512]{1,0:T(8,128)(2,1)S(1)}, bf16[224,512]{1,0:T(8,128)(2,1)S(1)}, u32[]{:S(2)}, u32[]{:S(2)}) collective-permute-start(bf16[224,512]{1,0:T(8,128)(2,1)S(1)} %collective-permute-done.9), channel_id=1, source_target_pairs={{0,2},{2,4},{4,6},{6,8},{8,10},{10,12},{12,14},{14,0},{1,3},{3,5},... | collective-permute-start | bytes 688136 | tf_op jit(solution)/shard_map/ppermute | solution.py:37
  86.1 6.1 %collective-permute-start.8 = (bf16[224,512]{1,0:T(8,128)(2,1)S(1)}, bf16[224,512]{1,0:T(8,128)(2,1)S(1)}, u32[]{:S(2)}, u32[]{:S(2)}) collective-permute-start(bf16[224,512]{1,0:T(8,128)(2,1)S(1)} %collective-permute-done.7), channel_id=1, source_target_pairs={{0,14},{2,0},{4,2},{6,4},{8,6},{10,8},{12,10},{14,12},{1,15},{3,1}... | collective-permute-start | bytes 688136 | tf_op jit(solution)/shard_map/ppermute | solution.py:37
  92.2 5.2 %collective-permute-start.13 = (bf16[112,512]{1,0:T(8,128)(2,1)S(1)}, bf16[112,512]{1,0:T(8,128)(2,1)S(1)}, u32[]{:S(2)}, u32[]{:S(2)}) collective-permute-start(bf16[112,512]{1,0:T(8,128)(2,1)S(1)} %slice.263), channel_id=1, source_target_pairs={{0,14},{2,0},{4,2},{6,4},{8,6},{10,8},{12,10},{14,12},{1,15},{3,1}... | collective-permute-start | bytes 344072 | tf_op jit(solution)/shard_map/ppermute | solution.py:37
  94.9 4.9 %collective-permute-start.14 = (bf16[112,512]{1,0:T(8,128)(2,1)S(1)}, bf16[112,512]{1,0:T(8,128)(2,1)S(1)}, u32[]{:S(2)}, u32[]{:S(2)}) collective-permute-start(bf16[112,512]{1,0:T(8,128)(2,1)S(1)} %slice.264), channel_id=1, source_target_pairs={{0,2},{2,4},{4,6},{6,8},{8,10},{10,12},{12,14},{14,0},{1,3},{3,5},... | collective-permute-start | bytes 344072 | tf_op jit(solution)/shard_map/ppermute | solution.py:37
  100.0 9.6 %copy-start.16 = (f32[224,5]{1,0:T(8,128)S(1)}, f32[224,5]{1,0:T(8,128)}, u32[]{:S(2)}) copy-start(f32[224,5]{1,0:T(8,128)} %constant.79.clone.1) | copy-start | bytes 13444
  105.3 4.4 %collective-permute-start.16 = (f32[224,5]{1,0:T(8,128)S(1)}, f32[224,5]{1,0:T(8,128)S(1)}, u32[]{:S(2)}, u32[]{:S(2)}) collective-permute-start(f32[224,5]{1,0:T(8,128)S(1)} %slice_select_fusion), channel_id=1, source_target_pairs={{0,16},{16,0},{1,17},{17,1},{2,18},{18,2},{3,19},{19,3},{4,20},{20... | collective-permute-start | bytes 13448 | tf_op jit(solution)/shard_map/ppermute | solution.py:33
  110.4 12.2 %collective-permute-start.27 = (bf16[224,128]{1,0:T(8,128)(2,1)S(1)}, bf16[224,128]{1,0:T(8,128)(2,1)S(1)}, u32[]{:S(2)}, u32[]{:S(2)}) collective-permute-start(bf16[224,128]{1,0:T(8,128)(2,1)S(1)} %slice.475), channel_id=1, source_target_pairs={{0,16},{1,17},{2,18},{3,19},{4,20},{5,21},{6,22},{7,23},{8,24},{9,... | collective-permute-start | bytes 172040 | tf_op jit(solution)/shard_map/ppermute | solution.py:255
  118.5 17.4 %collective-permute-start.23 = (bf16[224,256]{1,0:T(8,128)(2,1)S(1)}, bf16[224,256]{1,0:T(8,128)(2,1)S(1)}, u32[]{:S(2)}, u32[]{:S(2)}) collective-permute-start(bf16[224,256]{1,0:T(8,128)(2,1)S(1)} %slice.474), channel_id=1, source_target_pairs={{0,16},{1,17},{2,18},{3,19},{4,20},{5,21},{6,22},{7,23},{8,24},{9,... | collective-permute-start | bytes 344072 | tf_op jit(solution)/shard_map/ppermute | solution.py:255
  119.9 13.0 %collective-permute-start.17 = (bf16[112,256]{1,0:T(8,128)(2,1)S(1)}, bf16[112,256]{1,0:T(8,128)(2,1)S(1)}, u32[]{:S(2)}, u32[]{:S(2)}) collective-permute-start(bf16[112,256]{1,0:T(8,128)(2,1)S(1)} %get-tuple-element.100), channel_id=1, source_target_pairs={{0,2},{2,4},{4,6},{6,8},{8,10},{10,12},{12,14},{14,0},{1,3},{3,5},... | collective-permute-start | bytes 172040 | tf_op jit(solution)/shard_map/ppermute | solution.py:37
  120.0 12.9 %collective-permute-start.20 = (bf16[112,256]{1,0:T(8,128)(2,1)S(1)}, bf16[112,256]{1,0:T(8,128)(2,1)S(1)}, u32[]{:S(2)}, u32[]{:S(2)}) collective-permute-start(bf16[112,256]{1,0:T(8,128)(2,1)S(1)} %get-tuple-element.98), channel_id=1, source_target_pairs={{0,14},{2,0},{4,2},{6,4},{8,6},{10,8},{12,10},{14,12},{1,15},{3,1}... | collective-permute-start | bytes 172040 | tf_op jit(solution)/shard_map/ppermute | solution.py:37
  123.0 20.6 %collective-permute-start.28 = (bf16[112,3072]{1,0:T(8,128)(2,1)S(1)}, bf16[112,3072]{1,0:T(8,128)(2,1)S(1)}, u32[]{:S(2)}, u32[]{:S(2)}) collective-permute-start(bf16[112,3072]{1,0:T(8,128)(2,1)S(1)} %convolution_convert_fusion.2), channel_id=1, source_target_pairs={{0,1},{1,0},{2,3},{3,2},{4,5},{5,4},{6,7},{7,6},{8,9},{9,8},{10,11... | collective-permute-start | bytes 2064392 | tf_op jit(solution)/shard_map/ppermute | solution.py:33
  133.0 5.6 %collective-permute-start.18 = (bf16[224,256]{1,0:T(8,128)(2,1)S(1)}, bf16[224,256]{1,0:T(8,128)(2,1)S(1)}, u32[]{:S(2)}, u32[]{:S(2)}) collective-permute-start(bf16[224,256]{1,0:T(8,128)(2,1)S(1)} %pad_maximum_fusion.13), channel_id=1, source_target_pairs={{0,2},{2,4},{4,6},{6,8},{8,10},{10,12},{12,14},{14,0},{1,3},{3,5},... | collective-permute-start | bytes 344072 | tf_op jit(solution)/shard_map/ppermute | solution.py:37
  133.1 10.5 %copy-start.10 = (bf16[1,112,3072]{2,1,0:T(8,128)(2,1)S(1)}, bf16[1,112,3072]{2,1,0:T(8,128)(2,1)}, u32[]{:S(2)}) copy-start(bf16[1,112,3072]{2,1,0:T(8,128)(2,1)} %param.11) | copy-start | bytes 2064388
  133.1 5.5 %collective-permute-start.21 = (bf16[224,256]{1,0:T(8,128)(2,1)S(1)}, bf16[224,256]{1,0:T(8,128)(2,1)S(1)}, u32[]{:S(2)}, u32[]{:S(2)}) collective-permute-start(bf16[224,256]{1,0:T(8,128)(2,1)S(1)} %pad_maximum_fusion.14), channel_id=1, source_target_pairs={{0,14},{2,0},{4,2},{6,4},{8,6},{10,8},{12,10},{14,12},{1,15},{3,1}... | collective-permute-start | bytes 344072 | tf_op jit(solution)/shard_map/ppermute | solution.py:37
  136.2 11.0 %collective-permute-start.24 = (bf16[112,3072]{1,0:T(8,128)(2,1)S(1)}, bf16[112,3072]{1,0:T(8,128)(2,1)S(1)}, u32[]{:S(2)}, u32[]{:S(2)}) collective-permute-start(bf16[112,3072]{1,0:T(8,128)(2,1)S(1)} %convolution_convert_fusion.3), channel_id=1, source_target_pairs={{0,1},{1,0},{2,3},{3,2},{4,5},{5,4},{6,7},{7,6},{8,9},{9,8},{10,11... | collective-permute-start | bytes 2064392 | tf_op jit(solution)/shard_map/ppermute | solution.py:33
  138.6 4.9 %collective-permute-start.19 = (bf16[224,256]{1,0:T(8,128)(2,1)S(1)}, bf16[224,256]{1,0:T(8,128)(2,1)S(1)}, u32[]{:S(2)}, u32[]{:S(2)}) collective-permute-start(bf16[224,256]{1,0:T(8,128)(2,1)S(1)} %get-tuple-element.90), channel_id=1, source_target_pairs={{0,2},{2,4},{4,6},{6,8},{8,10},{10,12},{12,14},{14,0},{1,3},{3,5},... | collective-permute-start | bytes 344072 | tf_op jit(solution)/shard_map/ppermute | solution.py:37
  138.7 8.5 %copy-start.11 = (bf16[1,112,3072]{2,1,0:T(8,128)(2,1)S(1)}, bf16[1,112,3072]{2,1,0:T(8,128)(2,1)}, u32[]{:S(2)}) copy-start(bf16[1,112,3072]{2,1,0:T(8,128)(2,1)} %param.14) | copy-start | bytes 2064388
  138.7 4.8 %collective-permute-start.22 = (bf16[224,256]{1,0:T(8,128)(2,1)S(1)}, bf16[224,256]{1,0:T(8,128)(2,1)S(1)}, u32[]{:S(2)}, u32[]{:S(2)}) collective-permute-start(bf16[224,256]{1,0:T(8,128)(2,1)S(1)} %get-tuple-element.89), channel_id=1, source_target_pairs={{0,14},{2,0},{4,2},{6,4},{8,6},{10,8},{12,10},{14,12},{1,15},{3,1}... | collective-permute-start | bytes 344072 | tf_op jit(solution)/shard_map/ppermute | solution.py:37
  144.0 16.8 %copy-start.4 = (bf16[224,3072]{1,0:T(8,128)(2,1)S(1)}, bf16[224,3072]{1,0:T(8,128)(2,1)}, u32[]{:S(2)}) copy-start(bf16[224,3072]{1,0:T(8,128)(2,1)} %copy-done.3) | copy-start | bytes 4128772
  144.0 16.0 %collective-permute-start.29 = (bf16[112,3072]{1,0:T(8,128)(2,1)S(1)}, bf16[112,3072]{1,0:T(8,128)(2,1)S(1)}, u32[]{:S(2)}, u32[]{:S(2)}) collective-permute-start(bf16[112,3072]{1,0:T(8,128)(2,1)S(1)} %fusion.3), channel_id=1, source_target_pairs={{0,32},{32,64},{64,96},{96,128},{128,160},{160,192},{192,224},{1,3... | collective-permute-start | bytes 2064392 | tf_op jit(solution)/shard_map/ppermute | solution.py:27
  148.5 4.9 %collective-permute-start.25 = (bf16[224,256]{1,0:T(8,128)(2,1)S(1)}, bf16[224,256]{1,0:T(8,128)(2,1)S(1)}, u32[]{:S(2)}, u32[]{:S(2)}) collective-permute-start(bf16[224,256]{1,0:T(8,128)(2,1)S(1)} %get-tuple-element.66), channel_id=1, source_target_pairs={{0,2},{2,4},{4,6},{6,8},{8,10},{10,12},{12,14},{14,0},{1,3},{3,5},... | collective-permute-start | bytes 344072 | tf_op jit(solution)/shard_map/ppermute | solution.py:37
  149.6 3.7 %collective-permute-start.26 = (bf16[224,256]{1,0:T(8,128)(2,1)S(1)}, bf16[224,256]{1,0:T(8,128)(2,1)S(1)}, u32[]{:S(2)}, u32[]{:S(2)}) collective-permute-start(bf16[224,256]{1,0:T(8,128)(2,1)S(1)} %get-tuple-element.67), channel_id=1, source_target_pairs={{0,14},{2,0},{4,2},{6,4},{8,6},{10,8},{12,10},{14,12},{1,15},{3,1}... | collective-permute-start | bytes 344072 | tf_op jit(solution)/shard_map/ppermute | solution.py:37
  160.0 0.8 copy-start.12
  166.3 8.6 %collective-permute-start.30 = (bf16[112,3072]{1,0:T(8,128)(2,1)}, bf16[112,3072]{1,0:T(8,128)(2,1)}, u32[]{:S(2)}, u32[]{:S(2)}) collective-permute-start(bf16[112,3072]{1,0:T(8,128)(2,1)} %convolution_convert_fusion.1), channel_id=1, source_target_pairs={{0,1},{1,0},{2,3},{3,2},{4,5},{5,4},{6,7},{7,6},{8,9},{9,8},{10,11... | collective-permute-start | bytes 2064392 | tf_op jit(solution)/shard_map/ppermute | solution.py:33
  171.7 5.5 %copy-start.2 = (bf16[1,112,3072]{2,1,0:T(8,128)(2,1)S(1)}, bf16[1,112,3072]{2,1,0:T(8,128)(2,1)}, u32[]{:S(2)}) copy-start(bf16[1,112,3072]{2,1,0:T(8,128)(2,1)} %param.13) | copy-start | bytes 2064388
  171.7 5.5 %copy-start.14 = (bf16[1,112,3072]{2,1,0:T(8,128)(2,1)S(1)}, bf16[1,112,3072]{2,1,0:T(8,128)(2,1)}, u32[]{:S(2)}) copy-start(bf16[1,112,3072]{2,1,0:T(8,128)(2,1)} %param.15) | copy-start | bytes 2064388
  171.7 21.8 %collective-permute-start.31 = (bf16[112,3072]{1,0:T(8,128)(2,1)}, bf16[112,3072]{1,0:T(8,128)(2,1)}, u32[]{:S(2)}, u32[]{:S(2)}) collective-permute-start(bf16[112,3072]{1,0:T(8,128)(2,1)} %fusion.2), channel_id=1, source_target_pairs={{32,0},{64,32},{96,64},{128,96},{160,128},{192,160},{224,192},{33,... | collective-permute-start | bytes 2064392 | tf_op jit(solution)/shard_map/ppermute | solution.py:27
  178.8 29.3 %collective-permute-start.32 = (bf16[112,3072]{1,0:T(8,128)(2,1)S(1)}, bf16[112,3072]{1,0:T(8,128)(2,1)S(1)}, u32[]{:S(2)}, u32[]{:S(2)}) collective-permute-start(bf16[112,3072]{1,0:T(8,128)(2,1)S(1)} %fusion.17), channel_id=1, source_target_pairs={{32,0},{64,32},{96,64},{128,96},{160,128},{192,160},{224,192},{33,... | collective-permute-start | bytes 2064392 | tf_op jit(solution)/shard_map/ppermute | solution.py:27
  214.3 6.7 %copy-start.13 = (bf16[112,3072]{1,0:T(8,128)(2,1)S(1)}, bf16[112,3072]{1,0:T(8,128)(2,1)}, u32[]{:S(2)}) copy-start(bf16[112,3072]{1,0:T(8,128)(2,1)} %copy-done.12) | copy-start | bytes 2064388
  214.3 5.6 %collective-permute-start.33 = (bf16[2,96,512]{2,1,0:T(8,128)(2,1)S(1)}, bf16[2,96,512]{2,1,0:T(8,128)(2,1)S(1)}, u32[]{:S(2)}, u32[]{:S(2)}) collective-permute-start(bf16[2,96,512]{2,1,0:T(8,128)(2,1)S(1)} %get-tuple-element.111), channel_id=1, source_target_pairs={{0,1},{1,0},{2,3},{3,2},{4,5},{5,4},{6,7},{7,6},{8,9},{9,8},{10,11... | collective-permute-start | bytes 589832 | tf_op jit(solution)/shard_map/ppermute | solution.py:33
  219.9 6.6 %collective-permute-start.34 = (bf16[96,1024]{1,0:T(8,128)(2,1)S(1)}, bf16[96,1024]{1,0:T(8,128)(2,1)S(1)}, u32[]{:S(2)}, u32[]{:S(2)}) collective-permute-start(bf16[96,1024]{1,0:T(8,128)(2,1)S(1)} %select_bitcast_fusion.6), channel_id=1, source_target_pairs={{0,16},{16,0},{1,17},{17,1},{2,18},{18,2},{3,19},{19,3},{4,20},{20... | collective-permute-start | bytes 589832 | tf_op jit(solution)/shard_map/ppermute | solution.py:33
Sparse Core Ops, SparseCore 0:
  19.0 47.2 all-gather.2
  164.7 48.5 reduce-scatter.1
